TPU v7x, 256 devices: a whole 4x4x8 slice. The times are simulated.
256 devices in a mesh: row: 8 (over y, z_lo), col: 32 (over z_hi, x, core).
Axes of the slice: x: 4, y: 4, z: 8 (z_hi: 4, z_lo: 2; z = z_hi * 2 + z_lo), core: 2. Of those that a mesh axis runs over, the one named last changes fastest.
Arguments:
- positions: float32 [3, 524288], P(None, ('row', 'col')), may hold values from 0 to 173
- type_ids: int32 [524288], P(('row', 'col')), may hold values from 0 to 15
- type_params: float32 [2, 16], replicated, may hold values from 0.5 to 2
- pair_tiles: int32 [8, 32, 384, 2], P('row', 'col'), may hold values from 0 to 511, as said below
- pair_counts: int32 [8, 32], P('row', 'col'), may hold values from 48 to 384, as said below
Outputs:
- forces: float32 [3, 524288], P(None, ('row', 'col'))
Inputs may be any that keep to these rules, and one draw needn't show every extreme that they name: `pair_tiles`: column 0 is a tile of the device's row block (below 512), column 1 a tile of its column set (below 128); slots at or after the device's count hold indices to be ignored. `pair_counts`: some device has all 384 slots live.
All inputs are finite; a program needn't handle non-finite values.
Results may differ from a plain program's by a relative error of at most 0.0003.
Values sent between devices are 32-bit elements; how exact they have to be, the bound alone decides.
A program may use at most 128 MiB of HBM per device.

v0:
```python
import jax
import jax.numpy as jnp
from jax import lax
from jax.sharding import PartitionSpec as P

TILE = 128
NTYPES = 16


STRENGTH = 1.0
CUTOFF_SQ = 6.25
pair_batch = 32


def atom_table(positions, type_ids, type_params):
    onehot = (type_ids[None, :] == jnp.arange(NTYPES, dtype=jnp.int32)[:, None]).astype(jnp.float32)
    per_atom = jnp.dot(type_params, onehot, precision=lax.Precision.HIGHEST)
    return jnp.concatenate([positions, jnp.sqrt(per_atom[0:1]), per_atom[1:2]], axis=0)


def tile_split(atom_data):
    return atom_data.reshape(atom_data.shape[0], atom_data.shape[1] // TILE, TILE).transpose(
        1, 0, 2
    )


def tile_join(tiled):
    return tiled.transpose(1, 0, 2).reshape(tiled.shape[1], tiled.shape[0] * tiled.shape[2])


def pair_block(row_tiles, col_tiles, pair_list, live_slot):
    left_tile = row_tiles[pair_list[:, 0]]
    right_tile = col_tiles[pair_list[:, 1]]
    offset_vec = left_tile[:, :3, :, None] - right_tile[:, :3, None, :]
    dist_sq = jnp.sum(offset_vec * offset_vec, axis=1)
    well_depth = left_tile[:, 3, :, None] * right_tile[:, 3, None, :]
    well_width = 0.5 * (left_tile[:, 4, :, None] + right_tile[:, 4, None, :])
    inverse_sq = 1.0 / (well_width * well_width)
    falloff = jnp.exp(-dist_sq * inverse_sq)
    cutoff_term = jnp.maximum(1.0 - dist_sq / CUTOFF_SQ, 0.0)
    radial_slope = (
        STRENGTH
        * well_depth
        * falloff
        * (-cutoff_term * cutoff_term * inverse_sq - 2.0 * cutoff_term / CUTOFF_SQ)
    )
    radial_slope = jnp.where(live_slot[:, None, None], radial_slope, 0.0)
    pair_force = 2.0 * radial_slope[:, None] * offset_vec
    return (-jnp.sum(pair_force, axis=3), jnp.sum(pair_force, axis=2))


def evaluate(row_tiles, col_tiles, pair_tiles, slot_count, blocks):
    row_zero = jnp.zeros((row_tiles.shape[0], 3, TILE), jnp.float32)
    col_zero = jnp.zeros((col_tiles.shape[0], 3, TILE), jnp.float32)

    def block_step(block_id, totals):
        first_slot = jnp.asarray(block_id, jnp.int32) * pair_batch
        pair_list = lax.dynamic_slice_in_dim(pair_tiles, first_slot, pair_batch, 0)
        live_slot = first_slot + jnp.arange(pair_batch, dtype=jnp.int32) < slot_count
        on_rows, on_cols = pair_block(row_tiles, col_tiles, pair_list, live_slot)
        return (
            totals[0].at[pair_list[:, 0]].add(on_rows),
            totals[1].at[pair_list[:, 1]].add(on_cols),
        )

    return lax.fori_loop(0, blocks, block_step, (row_zero, col_zero))


def shards(positions, type_ids, type_params, pair_tiles, pair_counts):
    own_data = atom_table(positions, type_ids, type_params)
    row_data = lax.all_gather(own_data, "col", axis=1, tiled=True)
    col_data = lax.all_gather(own_data, "row", axis=1, tiled=True)
    pair_list = pair_tiles[0, 0]
    slot_count = pair_counts[0, 0]
    blocks = pair_list.shape[0] // pair_batch
    row_force, col_force = evaluate(
        tile_split(row_data), tile_split(col_data), pair_list, slot_count, blocks
    )
    row_part = tile_join(row_force)
    col_part = tile_join(col_force)
    forces = lax.psum_scatter(row_part, "col", scatter_dimension=1, tiled=True) + lax.psum_scatter(
        col_part, "row", scatter_dimension=1, tiled=True
    )
    return forces


def solution(mesh):
    placed = (
        P(None, ("row", "col")),
        P(("row", "col")),
        P(),
        P("row", "col", None, None),
        P("row", "col"),
    )
    return jax.shard_map(
        shards, mesh=mesh, in_specs=placed, out_specs=P(None, ("row", "col")), check_vma=False
    )
```

profile of v0, /device:TPU:1, one launch (start us, length us, event | category | flops | bytes accessed | tf_op | source)
XLA Modules:
  0.0 708.1 jit_solution(5086100597955837674)
XLA Ops:
  9.6 26.2 %all_gather.7 = f32[5,16384]{1,0:T(8,128)S(1)} all-gather(f32[5,2048]{1,0:T(8,128)} %pad_maximum_fusion), channel_id=1, replica_groups=mesh['row'=8,'col'=32] {'row'}, dimensions={1}, use_global_device_ids=true | all-gather | bytes 368640 | tf_op jit(solution)/shard_map/all_gather | solution.py:72
  35.8 33.1 %all-gather.2.cloned.1.call-done = f32[5,65536]{1,0:T(8,128)} async-done(((f32[5,2048]{1,0:T(8,128)}), f32[5,65536]{1,0:T(8,128)}) %all-gather.2.cloned.1.call-update) | async-done | bytes 1310736 | tf_op jit(solution)/shard_map/all_gather | solution.py:71
  69.1 188.8 %while.17 = (s32[]{:T(128)}, f32[512,3,128]{2,1,0:T(4,128)S(1)}, f32[128,3,128]{2,1,0:T(4,128)S(1)}, s32[384,2]{0,1:T(2,128)}, s32[]{:T(128)}, /*index=5*/f32[51...) while((s32[]{:T(128)}, f32[512,3,128]{2,1,0:T(4,128)S(1)}, ...), condition=%wide.region_6.7_spmd, body=%wide.region_0.6_spmd.sunk | while | flops 20461828 | bytes 9807847 | solution.py:66
  71.2 2.2 gather_fusion.1
  73.5 2.1 fusion.21
  75.5 1.9 fusion.24
  77.5 4.0 fusion.25
  81.6 1.6 scatter_fusion.1
  87.0 2.2 gather_fusion.1
  89.2 2.1 fusion.21
  91.3 1.9 fusion.24
  93.2 4.0 fusion.25
  97.3 1.6 scatter_fusion.1
  102.7 2.2 gather_fusion.1
  104.9 2.1 fusion.21
  107.0 1.9 fusion.24
  109.0 4.0 fusion.25
  114.7 1.6 scatter_fusion
  118.4 2.2 gather_fusion.1
  120.7 2.1 fusion.21
  122.7 1.9 fusion.24
  124.7 4.0 fusion.25
  128.8 1.6 scatter_fusion.1
  134.2 2.2 gather_fusion.1
  136.4 2.1 fusion.21
  138.5 1.9 fusion.24
  140.4 4.0 fusion.25
  144.5 1.6 scatter_fusion.1
  149.9 2.2 gather_fusion.1
  152.1 2.1 fusion.21
  154.2 1.9 fusion.24
  156.1 4.0 fusion.25
  165.6 2.2 gather_fusion.1
  167.8 2.1 fusion.21
  169.9 1.9 fusion.24
  171.9 4.0 fusion.25
  181.3 2.2 gather_fusion.1
  183.6 2.1 fusion.21
  185.6 1.9 fusion.24
  187.6 4.0 fusion.25
  197.1 2.2 gather_fusion.1
  199.3 2.1 fusion.21
  201.4 1.9 fusion.24
  203.3 4.0 fusion.25
  207.4 1.6 scatter_fusion.1
  212.8 2.2 gather_fusion.1
  215.0 2.1 fusion.21
  217.1 1.9 fusion.24
  219.0 4.0 fusion.25
  223.1 1.6 scatter_fusion.1
  228.5 2.2 gather_fusion.1
  230.8 2.1 fusion.21
  232.8 1.9 fusion.24
  234.8 4.0 fusion.25
  238.9 1.6 scatter_fusion.1
  244.3 2.2 gather_fusion.1
  246.5 2.1 fusion.21
  248.6 1.9 fusion.24
  250.5 4.0 fusion.25
  254.6 1.6 scatter_fusion.1
  257.9 5.0 copy.14
  263.0 16.1 %copy.12 = f32[3,65536]{0,1:T(8,128)} copy(f32[3,65536]{1,0:T(4,128)S(1)} %bitcast.41) | data formatting | bytes 1572864
  279.1 152.4 %reduce-scatter.9.cloned.1.call-done = f32[2048,3]{1,0:T(8,128)} async-done(((f32[16384,3]{1,0:T(8,128)}), f32[2048,3]{1,0:T(8,128)}) %reduce-scatter.9.cloned.1.call-update) | async-done | bytes 24592
  433.1 266.3 %reduce-scatter.7.cloned.1.call-done = f32[2048,3]{1,0:T(8,128)} async-done(((f32[65536,3]{1,0:T(8,128)}), f32[2048,3]{1,0:T(8,128)}) %reduce-scatter.7.cloned.1.call-update) | async-done | bytes 24592
  (151 shorter events, 56.9 us)
Async XLA Ops:
  6.5 0.7 copy-start
  6.5 62.4 %all-gather.2.cloned.1.call-start = ((), (), s32[]{:S(2)}) async-start(), calls=%async_computation.2 | async-start | bytes 2162688 | tf_op jit(solution)/shard_map/all_gather | solution.py:71
  9.5 422.0 %reduce-scatter.9.cloned.1.call-start = ((), (), s32[]{:S(2)}) async-start(), calls=%async_computation.4 | async-start | bytes 9437184
  262.9 436.5 %reduce-scatter.7.cloned.1.call-start = ((), (), s32[]{:S(2)}) async-start(), calls=%async_computation.3 | async-start | bytes 34603008
Sparse Core Ops, SparseCore 0:
  9.9 58.9 all-gather.1
  263.1 168.4 reduce-scatter.8
  435.7 263.6 reduce-scatter.6
where the time goes:
time: 709 us; the launch traced here: 708 us
  waiting for transfers between devices  452 us (64%)
  other arithmetic  146 us (21%)
  local copies, waits for them, and re-layouts  68.1 us (10%)
  blocking collectives  26.2 us (4%)
  between operations  13.1 us (2%)
    unnamed x5, waiting for transfers between devices  419 us
    reduce_sum x12, other arithmetic, pair_block(): return (-jnp.sum(pair_force, axis=3), jnp.sum(pair_force, axis=2))  48.5 us
    all_gather x1, waiting for transfers between devices, shards(): row_data = lax.all_gather(own_data, 'col', axis=1, tiled=True)  33.1 us
    all_gather x1, blocking collectives, shards(): col_data = lax.all_gather(own_data, 'row', axis=1, tiled=True)  26.2 us
    gather x12, local copies, waits for them, and re-layouts, pair_block(): left_tile = row_tiles[pair_list[:, 0]]  25.9 us
    unnamed x6, local copies, waits for them, and re-layouts  24.9 us
    reduce_sum x12, other arithmetic, pair_block(): dist_sq = jnp.sum(offset_vec * offset_vec, axis=1)  24.8 us
    mul x12, other arithmetic, pair_block(): pair_force = 2.0 * radial_slope[:, None] * offset_vec  23.3 us
  transfers between devices with their start and end apart: 3, of which 3 were waited for; matrix products, arithmetic and copies ran while one was open for 2% of the time, Pallas kernels for 0%

commit v1 on v0

v1 whole, which is shorter than its diff:
```python
import functools
import math

import jax
import jax.numpy as jnp
from jax import lax
from jax.experimental import pallas as pl
from jax.experimental.pallas import tpu as pltpu
from jax.sharding import PartitionSpec as P

TILE = 128
NTYPES = 16
CUTOFF_SQ = 6.25
LOG2E = math.log2(math.e)
KAPPA = 2.0 / (CUTOFF_SQ * LOG2E)
UNROLL = 2
ROW_TILES = 512
COL_TILES = 128
F32 = jnp.float32
BF16 = jnp.bfloat16


def pieces(value):
    high = value.astype(BF16).astype(F32)
    rest = value - high
    middle = rest.astype(BF16).astype(F32)
    return high, middle, rest, rest - middle


def distance_stack(value, order):
    high, middle, _, low = pieces(value)
    part = {"h": high, "m": middle, "l": low}
    return [jnp.concatenate([part[order[k]], part[order[k + 1]]], axis=0).astype(BF16) for k in (0, 2, 4)]


def moment_stack(value, upper):
    high, _, rest, low = pieces(value)
    return jnp.concatenate([jnp.where(upper, high, rest), jnp.where(upper, low, 0.0)], axis=0).astype(BF16)


def force_kernel(count_ref, tiles_ref, params_ref, row_ref, col_ref, row_out, col_out, feat, mom, cen, vel, acc_row, acc_col):
    sub = lax.broadcasted_iota(jnp.int32, (8, TILE), 0)
    quad = sub & 3
    upper = sub < 4
    subf = sub.astype(F32)
    unit = jnp.where(sub == 4, 1.0, 0.0)

    eye = lax.broadcasted_iota(jnp.int32, (NTYPES, NTYPES), 0) == lax.broadcasted_iota(jnp.int32, (NTYPES, NTYPES), 1)
    width = params_ref[1:2, :]
    width_sub = jnp.sum(jnp.where(eye, width, 0.0), axis=1, keepdims=True)
    total = 0.5 * (width_sub + width)
    table = (CUTOFF_SQ * LOG2E) / (total * total)
    t_high, t_mid, _, t_low = pieces(table)
    table48 = jnp.concatenate([t_high, t_mid, t_low], axis=0).astype(BF16)
    root = jnp.sqrt(params_ref[0:1, :])
    root_sub = jnp.sum(jnp.where(eye, root, 0.0), axis=1, keepdims=True)
    root_a = jnp.broadcast_to(root_sub[0:8], (8, TILE))
    root_b = jnp.broadcast_to(root_sub[8:16], (8, TILE))

    def typed(kind):
        hit_a = subf == kind
        hit_b = subf + 8.0 == kind
        onehot = jnp.concatenate([jnp.where(hit_a, 1.0, 0.0), jnp.where(hit_b, 1.0, 0.0)], axis=0).astype(BF16)
        depth = jnp.sum(jnp.where(hit_a, root_a, 0.0) + jnp.where(hit_b, root_b, 0.0), axis=0, keepdims=True)
        return onehot, jnp.broadcast_to(depth, (8, TILE))

    def spread(x, y, z, last):
        return jnp.where(quad == 0, x, jnp.where(quad == 1, y, jnp.where(quad == 2, z, last)))

    def wide(ref, dev, comp, lane):
        return jnp.broadcast_to(ref[dev, comp : comp + 1, pl.ds(lane, TILE)], (8, TILE))

    zero_pack = jnp.zeros((16, TILE), BF16)

    def prepare(b):
        dev = b // 16
        lane = pl.multiple_of((b % 16) * TILE, TILE)
        x, y, z, kind = (wide(col_ref, dev, k, lane) for k in range(4))
        here = spread(x, y, z, 0.0)
        centre = jnp.sum(here, axis=1, keepdims=True) * (1.0 / TILE)
        cen[b] = jnp.broadcast_to(centre, (8, TILE))
        v = here - centre
        square = jnp.where(sub < 3, v * v, 0.0)
        norm = jnp.sum(square, axis=0, keepdims=True)
        onehot, depth = typed(kind)
        z8 = jnp.where(sub < 3, v * (2.0 / CUTOFF_SQ), jnp.where(sub == 3, 1.0, jnp.where(sub == 4, norm * (-1.0 / CUTOFF_SQ), 0.0)))
        first = distance_stack(z8, "hmlhmh")
        second = jnp.dot(table48, onehot, preferred_element_type=F32).astype(BF16)
        stack = jnp.concatenate(first + [second, zero_pack, zero_pack], axis=0)
        feat[b] = stack.T
        xz = jnp.where(quad == 3, 1.0, v)
        mom[b] = moment_stack(xz * depth, upper)
        vel[b] = jnp.where(sub == 3, depth * KAPPA, v)

    @pl.loop(0, COL_TILES, step=4)
    def _(b0):
        for k in range(4):
            prepare(b0 + k)

    acc_row[...] = jnp.zeros_like(acc_row)
    acc_col[...] = jnp.zeros_like(acc_col)

    count = count_ref[0, 0]

    def fold(out):
        first = out[0:8]
        return first + pltpu.roll(first, 4, 0) + out[8:16]

    def pair(slot):
        live = slot < count
        a = jnp.where(live, tiles_ref[0, slot], 0)
        b = jnp.where(live, tiles_ref[1, slot], 0)
        a_to = pl.multiple_of(jnp.where(live, a, ROW_TILES) * 8, 8)
        b_to = pl.multiple_of(jnp.where(live, b, COL_TILES) * 8, 8)
        owner = a // 16
        dev = (owner & 1) * 16 + ((owner >> 1) & 3) * 4 + (owner >> 3)
        lane = pl.multiple_of((a & 15) * TILE, TILE)
        x, y, z = (wide(row_ref, dev, k, lane) - jnp.broadcast_to(cen[b, k : k + 1, :], (8, TILE)) for k in range(3))
        kind = wide(row_ref, dev, 3, lane)
        onehot, depth = typed(kind)
        q = 1.0 - (x * x + y * y + z * z) * (1.0 / CUTOFF_SQ)
        xz = spread(x, y, z, 1.0)
        z8 = jnp.where(sub < 3, xz, jnp.where(sub == 3, q, unit))
        blocks = distance_stack(z8, "hhhmml")
        zeros3 = [zero_pack] * 3
        near = jnp.concatenate(blocks + zeros3 + [zero_pack] * 2, axis=0)
        kinds = jnp.concatenate(zeros3 + [onehot] * 3 + [zero_pack] * 2, axis=0)
        both = jnp.dot(feat[b], jnp.concatenate([near, kinds], axis=1), preferred_element_type=F32)
        c = jnp.maximum(both[:, :TILE], 0.0)
        k = both[:, TILE:]
        u = c * k
        g = (c * (u + 2.0 * LOG2E)) * jnp.exp2(u - k)
        g_high = g.astype(BF16)
        g_low = (g - g_high.astype(F32)).astype(BF16)
        xj = mom[b]
        xi = moment_stack(xz * depth, upper)
        to_i = fold(jnp.dot(xj, g_high, preferred_element_type=F32) + jnp.dot(xj, g_low, preferred_element_type=F32))
        across = (((1,), (1,)), ((), ()))
        to_j = fold(
            lax.dot_general(xi, g_high, across, preferred_element_type=F32)
            + lax.dot_general(xi, g_low, across, preferred_element_type=F32)
        )
        weight = jnp.broadcast_to(to_i[3:4], (8, TILE))
        on_i = (xz * weight - to_i) * (depth * KAPPA)
        return a_to, b_to, on_i, to_j

    @pl.loop(0, pl.cdiv(count, UNROLL))
    def _(step):
        done = [pair(step * UNROLL + k) for k in range(UNROLL)]
        for a_to, b_to, on_i, to_j in done:
            acc_row[pl.ds(a_to, 8), :] += on_i
            acc_col[pl.ds(b_to, 8), :] += to_j

    @pl.loop(0, COL_TILES, step=4)
    def _(b0):
        for k in range(4):
            b = b0 + k
            at = pl.multiple_of(b * 8, 8)
            got = acc_col[pl.ds(at, 8), :]
            v = vel[b]
            weight = jnp.broadcast_to(got[3:4], (8, TILE))
            depth = jnp.broadcast_to(v[3:4], (8, TILE))
            acc_col[pl.ds(at, 8), :] = (v * weight - got) * depth

    for q in range(32):
        slot = (q & 1) * 16 + ((q >> 1) & 3) * 4 + (q >> 3)
        for c in range(3):
            row_out[slot, c * 16 : c * 16 + 16, :] = acc_row[pl.ds(q * 128 + c, 16, stride=8), :]
    for p in range(8):
        for c in range(3):
            col_out[p, c * 16 : c * 16 + 16, :] = acc_col[pl.ds(p * 128 + c, 16, stride=8), :]


def forces_of(count, tiles, params, row_data, col_data):
    smem = pl.BlockSpec(memory_space=pltpu.SMEM)
    vmem = pl.BlockSpec(memory_space=pltpu.VMEM)
    return pl.pallas_call(
        force_kernel,
        out_shape=(jax.ShapeDtypeStruct((32, 48, TILE), F32), jax.ShapeDtypeStruct((8, 48, TILE), F32)),
        in_specs=[smem, smem, vmem, vmem, vmem],
        out_specs=(vmem, vmem),
        scratch_shapes=[
            pltpu.VMEM((COL_TILES, TILE, TILE), BF16),
            pltpu.VMEM((COL_TILES, 16, TILE), BF16),
            pltpu.VMEM((COL_TILES, 8, TILE), F32),
            pltpu.VMEM((COL_TILES, 8, TILE), F32),
            pltpu.VMEM(((ROW_TILES + 1) * 8, TILE), F32),
            pltpu.VMEM(((COL_TILES + 1) * 8, TILE), F32),
        ],
        compiler_params=pltpu.CompilerParams(vmem_limit_bytes=40 * 1024 * 1024),
        name="pair_forces",
    )(count, tiles, params, row_data, col_data)


MESH = pl.DeviceIdType.MESH
HALF = 1024


def place():
    p, q = lax.axis_index("row"), lax.axis_index("col")
    return p // 2, p % 2, q // 8, (q // 2) % 4, q % 2


def device(y, zl, zh, x, core):
    return (y * 2 + zl, zh * 8 + x * 2 + core)


def neighbours(y, zl, zh, x, core):
    ring = lambda v, d: (v + d + 4) % 4
    return dict(
        z_up=device(y, zl, ring(zh, 1), x, core),
        z_down=device(y, zl, ring(zh, -1), x, core),
        x_up=device(y, zl, zh, ring(x, 1), core),
        x_down=device(y, zl, zh, ring(x, -1), core),
        y_up=device(ring(y, 1), zl, zh, x, core),
        y_down=device(ring(y, -1), zl, zh, x, core),
        twin=device(y, zl, zh, x, 1 - core),
        pal=device(y, 1 - zl, zh, x, core),
    )


def greet(near):
    barrier = pltpu.get_barrier_semaphore()
    for target in near.values():
        pl.semaphore_signal(barrier, inc=1, device_id=target, device_id_type=MESH)
    pl.semaphore_wait(barrier, len(near))


class Copies:
    def __init__(self, near, send_sem, recv_sem):
        self.near, self.send_sem, self.recv_sem = near, send_sem, recv_sem
        self.number = 0
        self.started = []

    def start(self, source, target, to):
        k = self.number
        self.number += 1
        copy = pltpu.make_async_remote_copy(
            src_ref=source,
            dst_ref=target,
            send_sem=self.send_sem.at[k],
            recv_sem=self.recv_sem.at[k],
            device_id=self.near[to],
            device_id_type=MESH,
        )
        copy.start()
        self.started.append(copy)
        return copy

    def finish(self):
        for copy in self.started:
            copy.wait_send()


GATHER_COPIES = 48
SCATTER_COPIES = 32


def gather_kernel(pos_ref, type_ref, row_ref, col_ref, send_sem, recv_sem):
    y, zl, zh, x, core = place()
    near = neighbours(y, zl, zh, x, core)
    ring = lambda v, d: (v + d + 4) % 4
    at = lambda xx, zz: core * 16 + xx * 4 + zz
    mine = at(x, zh)
    col_at = lambda yy, ll: yy * 2 + ll
    col_mine = col_at(y, zl)
    for ref, slot in ((row_ref, mine), (col_ref, col_mine)):
        ref[slot, 0:3, :] = pos_ref[...]
        for k in range(16):
            ref[slot, 3:4, k * TILE : (k + 1) * TILE] = type_ref[k : k + 1, :].astype(F32)
    greet(near)
    net = Copies(near, send_sem, recv_sem)
    low, high = pl.ds(0, HALF), pl.ds(HALF, HALF)

    def whole(ref, slot, to):
        return net.start(ref.at[slot], ref.at[slot], to)

    def part(ref, slot, lanes, to):
        return net.start(ref.at[slot, :, lanes], ref.at[slot, :, lanes], to)

    z_from_down = whole(row_ref, mine, "z_up")
    z_from_up = whole(row_ref, mine, "z_down")
    pal_copy = whole(col_ref, col_mine, "pal")
    y_from_down = [whole(col_ref, col_mine, "y_up")]
    y_from_up = [whole(col_ref, col_mine, "y_down")]
    x_from_down, x_from_up = [], []

    def along_x(slot):
        x_from_down.append(whole(row_ref, slot, "x_up"))
        x_from_up.append(whole(row_ref, slot, "x_down"))

    along_x(mine)
    twins = [whole(row_ref, mine, "twin")]
    z_from_down.wait_recv()
    z_low = part(row_ref, at(x, ring(zh, -1)), low, "z_up")
    along_x(at(x, ring(zh, -1)))
    z_from_up.wait_recv()
    z_high = part(row_ref, at(x, ring(zh, 1)), high, "z_down")
    along_x(at(x, ring(zh, 1)))
    pal_copy.wait_recv()
    y_from_down.append(whole(col_ref, col_at(y, 1 - zl), "y_up"))
    y_from_up.append(whole(col_ref, col_at(y, 1 - zl), "y_down"))
    twins.append(whole(row_ref, at(x, ring(zh, -1)), "twin"))
    twins.append(whole(row_ref, at(x, ring(zh, 1)), "twin"))

    x_low, x_high = [], []

    def onward(k, zz):
        x_from_down[k].wait_recv()
        x_low.append(part(row_ref, at(ring(x, -1), zz), low, "x_up"))
        x_from_up[k].wait_recv()
        x_high.append(part(row_ref, at(ring(x, 1), zz), high, "x_down"))
        twins.append(whole(row_ref, at(ring(x, -1), zz), "twin"))
        twins.append(whole(row_ref, at(ring(x, 1), zz), "twin"))

    onward(0, zh)
    z_low.wait_recv()
    z_high.wait_recv()
    along_x(at(x, ring(zh, 2)))
    twins.append(whole(row_ref, at(x, ring(zh, 2)), "twin"))

    y_low, y_high = [], []
    for k, ll in ((0, zl), (1, 1 - zl)):
        y_from_down[k].wait_recv()
        y_low.append(part(col_ref, col_at(ring(y, -1), ll), low, "y_up"))
        y_from_up[k].wait_recv()
        y_high.append(part(col_ref, col_at(ring(y, 1), ll), high, "y_down"))

    onward(1, ring(zh, -1))
    onward(2, ring(zh, 1))
    onward(3, ring(zh, 2))
    for k, d in enumerate((0, -1, 1, 2)):
        x_low[k].wait_recv()
        x_high[k].wait_recv()
        twins.append(whole(row_ref, at(ring(x, 2), ring(zh, d)), "twin"))
    for copy in y_low + y_high + twins:
        copy.wait_recv()
    net.finish()


def gather(positions, kinds):
    vmem = pl.BlockSpec(memory_space=pltpu.VMEM)
    return pl.pallas_call(
        gather_kernel,
        out_shape=(jax.ShapeDtypeStruct((32, 4, 2048), F32), jax.ShapeDtypeStruct((8, 4, 2048), F32)),
        in_specs=[vmem, vmem],
        out_specs=(vmem, vmem),
        scratch_shapes=[pltpu.SemaphoreType.DMA((GATHER_COPIES,)), pltpu.SemaphoreType.DMA((GATHER_COPIES,))],
        compiler_params=pltpu.CompilerParams(
            collective_id=0, has_side_effects=True, vmem_limit_bytes=16 * 1024 * 1024
        ),
        name="gather_atoms",
    )(positions, kinds)


def scatter_kernel(row_ref, col_ref, out_ref, from_twin, row_sum, x_half, x_whole, z_half, z_whole, y_half, y_whole, pal_in, col_sum, send_sem, recv_sem):
    y, zl, zh, x, core = place()
    near = neighbours(y, zl, zh, x, core)
    ring = lambda v, d: (v + d + 4) % 4
    greet(near)
    net = Copies(near, send_sem, recv_sem)

    offsets = (2, 1, -1, 0)
    twins = {}
    for d in offsets:
        there = pl.ds((1 - core) * 16 + ring(x, d) * 4, 4)
        twins[d] = net.start(row_ref.at[there], from_twin.at[pl.ds(ring(x, d) * 4, 4)], "twin")

    far = ring(y, 2) * 2
    y_low = net.start(col_ref.at[pl.ds(far, 1)], y_half.at[pl.ds(0, 1)], "y_up")
    y_high = net.start(col_ref.at[pl.ds(far + 1, 1)], y_half.at[pl.ds(1, 1)], "y_down")

    def join(d):
        twins[d].wait_recv()
        rows = pl.ds(ring(x, d) * 4, 4)
        row_sum[rows] = row_ref[pl.ds(core * 16 + ring(x, d) * 4, 4)] + from_twin[rows]

    join(2)
    far_x = ring(x, 2) * 4
    x_low = net.start(row_sum.at[pl.ds(far_x, 2)], x_half.at[pl.ds(0, 2)], "x_up")
    x_high = net.start(row_sum.at[pl.ds(far_x + 2, 2)], x_half.at[pl.ds(2, 2)], "x_down")

    y_low.wait_recv()
    up = ring(y, 1) * 2
    col_sum[0] = col_ref[up] + y_half[0]
    y_up0 = net.start(col_sum.at[0], y_whole.at[0], "y_up")
    y_up1 = net.start(col_ref.at[up + 1], y_whole.at[1], "y_up")
    y_high.wait_recv()
    down = ring(y, -1) * 2
    col_sum[1] = col_ref[down + 1] + y_half[1]
    y_down0 = net.start(col_ref.at[down], y_whole.at[2], "y_down")
    y_down1 = net.start(col_sum.at[1], y_whole.at[3], "y_down")

    join(1)
    up_x = ring(x, 1) * 4
    x_up1 = net.start(row_sum.at[pl.ds(up_x + 2, 2)], x_whole.at[pl.ds(2, 2)], "x_up")
    join(-1)
    down_x = ring(x, -1) * 4
    x_down0 = net.start(row_sum.at[pl.ds(down_x, 2)], x_whole.at[pl.ds(4, 2)], "x_down")
    x_low.wait_recv()
    row_sum[pl.ds(up_x, 2)] += x_half[0:2]
    x_up0 = net.start(row_sum.at[pl.ds(up_x, 2)], x_whole.at[pl.ds(0, 2)], "x_up")
    x_high.wait_recv()
    row_sum[pl.ds(down_x + 2, 2)] += x_half[2:4]
    x_down1 = net.start(row_sum.at[pl.ds(down_x + 2, 2)], x_whole.at[pl.ds(6, 2)], "x_down")
    join(0)

    for copy in (y_up0, y_up1, y_down0, y_down1):
        copy.wait_recv()
    here = y * 2
    col_sum[2] = col_ref[here + 1 - zl] + y_whole[1 - zl] + y_whole[3 - zl]
    pal_copy = net.start(col_sum.at[2], pal_in, "pal")
    col_sum[3] = col_ref[here + zl] + y_whole[zl] + y_whole[2 + zl]

    for copy in (x_up1, x_down0, x_up0, x_down1):
        copy.wait_recv()
    base = x * 4
    row_sum[pl.ds(base, 4)] += x_whole[0:4] + x_whole[4:8]

    z_far = base + ring(zh, 2)
    z_low = net.start(row_sum.at[z_far, pl.ds(0, 24)], z_half.at[0], "z_up")
    z_high = net.start(row_sum.at[z_far, pl.ds(24, 24)], z_half.at[1], "z_down")
    z_up, z_down = base + ring(zh, 1), base + ring(zh, -1)
    z_up1 = net.start(row_sum.at[z_up, pl.ds(24, 24)], z_whole.at[0, pl.ds(24, 24)], "z_up")
    z_down0 = net.start(row_sum.at[z_down, pl.ds(0, 24)], z_whole.at[1, pl.ds(0, 24)], "z_down")
    z_low.wait_recv()
    row_sum[z_up, 0:24] += z_half[0]
    z_up0 = net.start(row_sum.at[z_up, pl.ds(0, 24)], z_whole.at[0, pl.ds(0, 24)], "z_up")
    z_high.wait_recv()
    row_sum[z_down, 24:48] += z_half[1]
    z_down1 = net.start(row_sum.at[z_down, pl.ds(24, 24)], z_whole.at[1, pl.ds(24, 24)], "z_down")
    pal_copy.wait_recv()
    for copy in (z_up1, z_down0, z_up0, z_down1):
        copy.wait_recv()
    col_sum[3] = col_sum[3] + pal_in[...] + row_sum[base + zh] + z_whole[0] + z_whole[1]
    for c in range(3):
        for k in range(16):
            out_ref[c : c + 1, k * TILE : (k + 1) * TILE] = col_sum[3, c * 16 + k : c * 16 + k + 1, :]
    net.finish()


def scatter(row_part, col_part):
    vmem = pl.BlockSpec(memory_space=pltpu.VMEM)
    block = lambda n: pltpu.VMEM((n, 48, TILE), F32)
    return pl.pallas_call(
        scatter_kernel,
        out_shape=jax.ShapeDtypeStruct((3, 2048), F32),
        in_specs=[vmem, vmem],
        out_specs=vmem,
        scratch_shapes=[
            block(16),
            block(16),
            block(4),
            block(8),
            pltpu.VMEM((2, 24, TILE), F32),
            block(2),
            block(2),
            block(4),
            pltpu.VMEM((48, TILE), F32),
            block(4),
            pltpu.SemaphoreType.DMA((SCATTER_COPIES,)),
            pltpu.SemaphoreType.DMA((SCATTER_COPIES,)),
        ],
        compiler_params=pltpu.CompilerParams(
            collective_id=1, has_side_effects=True, vmem_limit_bytes=16 * 1024 * 1024
        ),
        name="scatter_forces",
    )(row_part, col_part)


def shards(positions, type_ids, type_params, pair_tiles, pair_counts):
    row_data, col_data = gather(positions, type_ids.reshape(16, TILE))
    tiles = pair_tiles[0, 0].T
    row_part, col_part = forces_of(pair_counts, tiles, type_params, row_data, col_data)
    return scatter(row_part, col_part)


def solution(mesh):
    placed = (
        P(None, ("row", "col")),
        P(("row", "col")),
        P(),
        P("row", "col", None, None),
        P("row", "col"),
    )
    return jax.shard_map(
        shards, mesh=mesh, in_specs=placed, out_specs=P(None, ("row", "col")), check_vma=False
    )
```

time: 709 us -> 153 us (0.22)
  waiting for transfers between devices: 452 us -> 0 us
  Pallas kernels: 0 us -> 147 us
  other arithmetic: 146 us -> 0 us
  local copies, waits for them, and re-layouts: 68.1 us -> 2.74 us
  blocking collectives: 26.2 us -> 0 us
  between operations: 13.1 us -> 0.7 us
    unnamed x5 -> x0, waiting for transfers between devices: 419 us -> none
    pallas_call x0 -> x3, Pallas kernels: none -> 147 us  [the longest x1 101 us: scatter(): pl.pallas_call(scatter_kernel, out_shape=jax.ShapeDtypeStruct((3, 2048),...]
    reduce_sum x24 -> x0, other arithmetic: 73.3 us -> none  [the longest x12 48.5 us: pair_block(): return (-jnp.sum(pair_force, axis=3), jnp.sum(pair_force, axis=2))]
    scatter-add x24 -> x0, other arithmetic: 39.4 us -> none  [the longest x12 19.7 us: block_step(): totals[1].at[pair_list[:, 1]].add(on_cols)]
    all_gather x1 -> x0, waiting for transfers between devices: 33.1 us -> none  [shards(): row_data = lax.all_gather(own_data, 'col', axis=1, tiled=True)]
    gather x24 -> x0, local copies, waits for them, and re-layouts: 32.9 us -> none  [the longest x12 25.9 us: pair_block(): left_tile = row_tiles[pair_list[:, 0]]]
    all_gather x1 -> x0, blocking collectives: 26.2 us -> none  [shards(): col_data = lax.all_gather(own_data, 'row', axis=1, tiled=True)]
    mul x12 -> x0, other arithmetic: 23.3 us -> none  [pair_block(): pair_force = 2.0 * radial_slope[:, None] * offset_vec]
  transfers between devices with their start and end apart: 3 -> 0, of which waited for: 3 -> 0; matrix products, arithmetic and copies ran while one was open for 2% -> 0% of each run, Pallas kernels for 0% -> 0%
where the time goes in v1:
time: 153 us; the launch traced here: 151 us
  Pallas kernels  147 us (96%)
  local copies, waits for them, and re-layouts  2.74 us (2%)
    pallas_call x1, Pallas kernels, scatter(): pl.pallas_call(scatter_kernel, out_shape=jax.ShapeDtypeStruct((3, 2048),...  101 us
    pallas_call x1, Pallas kernels, gather(): pl.pallas_call(gather_kernel, out_shape=(jax.ShapeDtypeStruct((32, 4, 204...  25.3 us
    pallas_call x1, Pallas kernels, forces_of(): pl.pallas_call(force_kernel, out_shape=(jax.ShapeDtypeStruct((32, 48, TIL...  20.8 us

profile of v1, /device:TPU:1, one launch (start us, length us, event | category | flops | bytes accessed | tf_op | source)
XLA Modules:
  0.0 150.6 jit_solution(11362013688877613643)
XLA Ops:
  0.7 0.0 copy-start
  0.7 0.7 copy-done
  1.4 0.0 copy-start.1
  1.4 0.7 copy-done.1
  2.1 0.0 copy-start.3
  2.1 25.3 %gather_atoms.1 = (f32[32,4,2048]{2,1,0:T(4,128)S(1)}, f32[8,4,2048]{2,1,0:T(4,128)S(1)}) custom-call(f32[3,2048]{1,0:T(4,128)S(1)} %copy-done, s32[16,128]{1,0:T(8,128)S(1)} %bitcast.4), custom_call_target="tpu_custom_call" | custom-call | tf_op jit(solution)/shard_map/gather_atoms/pallas_call | solution.py:343
  27.4 0.0 copy-start.2
  27.4 0.0 copy-done.3
  27.4 0.7 copy-done.2
  28.1 20.8 %pair_forces.1 = (f32[32,48,128]{2,1,0:T(8,128)S(1)}, f32[8,48,128]{2,1,0:T(8,128)S(1)}) custom-call(s32[1,1]{1,0:T(1,128)S(6)} %copy.7.count_ref, s32[2,384]{1,0:T(2,128)S(1)} %bitcast.5, f32[2,16]{1,0:T(2,128)S(1)} %copy-done.3, f32[32,4,2048]{2,1,0:T(4,128)S(1)} %get-tuple-element.9.row_ref, f32[8,4,2048]{2,1,0:T(4,128)S(1)} %get-tuple-element.10.col_ref), custom_call_target="tpu_custom_call" | custom-call | tf_op jit(solution)/shard_map/pair_forces/pallas_call | solution.py:177
  48.9 101.1 %scatter_forces.1 = f32[3,2048]{1,0:T(4,128)S(1)} custom-call(f32[32,48,128]{2,1,0:T(8,128)S(1)} %get-tuple-element.11.row_ref, f32[8,48,128]{2,1,0:T(8,128)S(1)} %get-tuple-element.12.col_ref), custom_call_target="tpu_custom_call" | custom-call | tf_op jit(solution)/shard_map/scatter_forces/pallas_call | solution.py:445
  149.9 0.6 copy.8
Async XLA Ops:
  0.7 0.8 copy-start
  1.4 0.7 copy-start.1
  2.1 25.3 %copy-start.3 = (f32[2,16]{1,0:T(2,128)S(1)}, f32[2,16]{1,0:T(2,128)}, u32[]{:S(2)}) copy-start(f32[2,16]{1,0:T(2,128)} %params_ref.1) | copy-start | bytes 388
  27.4 0.7 copy-start.2

commit v2 on v1

--- a/solution.py
+++ b/solution.py
@@ -13,7 +13,8 @@
 CUTOFF_SQ = 6.25
 LOG2E = math.log2(math.e)
 KAPPA = 2.0 / (CUTOFF_SQ * LOG2E)
-UNROLL = 2
+UNROLL = 16
+PREPARE = 16
 ROW_TILES = 512
 COL_TILES = 128
 F32 = jnp.float32
@@ -38,7 +39,7 @@
     return jnp.concatenate([jnp.where(upper, high, rest), jnp.where(upper, low, 0.0)], axis=0).astype(BF16)
 
 
-def force_kernel(count_ref, tiles_ref, params_ref, row_ref, col_ref, row_out, col_out, feat, mom, cen, vel, acc_row, acc_col):
+def force_kernel(count_ref, tiles_ref, params_ref, row_ref, col_ref, row_out, col_out, feat, mom, cen, vel, acc_row, acc_col, slope, mine, offset, scale):
     sub = lax.broadcasted_iota(jnp.int32, (8, TILE), 0)
     quad = sub & 3
     upper = sub < 4
@@ -91,14 +92,18 @@
         xz = jnp.where(quad == 3, 1.0, v)
         mom[b] = moment_stack(xz * depth, upper)
         vel[b] = jnp.where(sub == 3, depth * KAPPA, v)
-
-    @pl.loop(0, COL_TILES, step=4)
+        acc_row[pl.ds(pl.multiple_of(b * 32, 32), 32), :] = jnp.zeros((32, TILE), F32)
+        acc_col[pl.ds(pl.multiple_of(b * 8, 8), 8), :] = jnp.zeros((8, TILE), F32)
+
+    @pl.loop(0, COL_TILES, step=PREPARE)
     def _(b0):
-        for k in range(4):
+        for k in range(PREPARE):
             prepare(b0 + k)
 
-    acc_row[...] = jnp.zeros_like(acc_row)
-    acc_col[...] = jnp.zeros_like(acc_col)
+    slope[...] = jnp.zeros_like(slope)
+    mine[...] = jnp.zeros_like(mine)
+    offset[...] = jnp.zeros_like(offset)
+    scale[...] = jnp.zeros_like(scale)
 
     count = count_ref[0, 0]
 
@@ -106,47 +111,63 @@
         first = out[0:8]
         return first + pltpu.roll(first, 4, 0) + out[8:16]
 
-    def pair(slot):
-        live = slot < count
-        a = jnp.where(live, tiles_ref[0, slot], 0)
-        b = jnp.where(live, tiles_ref[1, slot], 0)
-        a_to = pl.multiple_of(jnp.where(live, a, ROW_TILES) * 8, 8)
-        b_to = pl.multiple_of(jnp.where(live, b, COL_TILES) * 8, 8)
+    zeros3 = [zero_pack] * 3
+    zeros2 = [zero_pack] * 2
+
+    def names(slot):
+        live = (slot >= 0) & (slot < count)
+        at = jnp.clip(slot, 0, count - 1)
+        return live, tiles_ref[0, at], tiles_ref[1, at]
+
+    def spread_out(slot, k):
+        _, a, b = names(slot)
         owner = a // 16
         dev = (owner & 1) * 16 + ((owner >> 1) & 3) * 4 + (owner >> 3)
         lane = pl.multiple_of((a & 15) * TILE, TILE)
-        x, y, z = (wide(row_ref, dev, k, lane) - jnp.broadcast_to(cen[b, k : k + 1, :], (8, TILE)) for k in range(3))
+        x, y, z = (wide(row_ref, dev, c, lane) - jnp.broadcast_to(cen[b, c : c + 1, :], (8, TILE)) for c in range(3))
         kind = wide(row_ref, dev, 3, lane)
         onehot, depth = typed(kind)
         q = 1.0 - (x * x + y * y + z * z) * (1.0 / CUTOFF_SQ)
         xz = spread(x, y, z, 1.0)
         z8 = jnp.where(sub < 3, xz, jnp.where(sub == 3, q, unit))
-        blocks = distance_stack(z8, "hhhmml")
-        zeros3 = [zero_pack] * 3
-        near = jnp.concatenate(blocks + zeros3 + [zero_pack] * 2, axis=0)
-        kinds = jnp.concatenate(zeros3 + [onehot] * 3 + [zero_pack] * 2, axis=0)
+        near = jnp.concatenate(distance_stack(z8, "hhhmml") + zeros3 + zeros2, axis=0)
+        kinds = jnp.concatenate(zeros3 + [onehot] * 3 + zeros2, axis=0)
         both = jnp.dot(feat[b], jnp.concatenate([near, kinds], axis=1), preferred_element_type=F32)
         c = jnp.maximum(both[:, :TILE], 0.0)
-        k = both[:, TILE:]
-        u = c * k
-        g = (c * (u + 2.0 * LOG2E)) * jnp.exp2(u - k)
+        decay = both[:, TILE:]
+        u = c * decay
+        g = (c * (u + 2.0 * LOG2E)) * jnp.exp2(u - decay)
         g_high = g.astype(BF16)
         g_low = (g - g_high.astype(F32)).astype(BF16)
-        xj = mom[b]
-        xi = moment_stack(xz * depth, upper)
-        to_i = fold(jnp.dot(xj, g_high, preferred_element_type=F32) + jnp.dot(xj, g_low, preferred_element_type=F32))
-        across = (((1,), (1,)), ((), ()))
-        to_j = fold(
-            lax.dot_general(xi, g_high, across, preferred_element_type=F32)
-            + lax.dot_general(xi, g_low, across, preferred_element_type=F32)
+        slope[k, 0:TILE, :] = g_high
+        slope[k, TILE : 2 * TILE, :] = g_low
+        mine[k] = moment_stack(xz * depth, upper)
+        offset[k] = xz
+        scale[k] = depth * KAPPA
+
+    def gather_in(slot, k):
+        live, a, b = names(slot)
+        a_to = pl.multiple_of(jnp.where(live, a, ROW_TILES) * 8, 8)
+        b_to = pl.multiple_of(jnp.where(live, b, COL_TILES) * 8, 8)
+        sides = jnp.concatenate([mom[b], mine[k]], axis=0)
+        g = slope[k]
+        across = jnp.concatenate([g[:TILE].T, g[TILE:].T], axis=0)
+        out = jnp.dot(
+            jnp.concatenate([sides, sides], axis=1),
+            jnp.concatenate([g, across], axis=1),
+            preferred_element_type=F32,
         )
+        to_i = fold(out[0:16, :TILE])
+        to_j = fold(out[16:32, TILE:])
         weight = jnp.broadcast_to(to_i[3:4], (8, TILE))
-        on_i = (xz * weight - to_i) * (depth * KAPPA)
+        on_i = (offset[k] * weight - to_i) * scale[k]
         return a_to, b_to, on_i, to_j
 
-    @pl.loop(0, pl.cdiv(count, UNROLL))
+    @pl.loop(0, pl.cdiv(count, UNROLL) + 1)
     def _(step):
-        done = [pair(step * UNROLL + k) for k in range(UNROLL)]
+        done = [gather_in((step - 1) * UNROLL + k, k) for k in range(UNROLL)]
+        for k in range(UNROLL):
+            spread_out(step * UNROLL + k, k)
         for a_to, b_to, on_i, to_j in done:
             acc_row[pl.ds(a_to, 8), :] += on_i
             acc_col[pl.ds(b_to, 8), :] += to_j
@@ -186,6 +207,10 @@
             pltpu.VMEM((COL_TILES, 8, TILE), F32),
             pltpu.VMEM(((ROW_TILES + 1) * 8, TILE), F32),
             pltpu.VMEM(((COL_TILES + 1) * 8, TILE), F32),
+            pltpu.VMEM((UNROLL, 2 * TILE, TILE), BF16),
+            pltpu.VMEM((UNROLL, 16, TILE), BF16),
+            pltpu.VMEM((UNROLL, 8, TILE), F32),
+            pltpu.VMEM((UNROLL, 8, TILE), F32),
         ],
         compiler_params=pltpu.CompilerParams(vmem_limit_bytes=40 * 1024 * 1024),
         name="pair_forces",

time: 153 us -> 73.8 us (0.48)
  the two profiles are of different devices: /device:TPU:1 before, /device:TPU:18 now
where the time goes in v2:
time: 73.8 us; the launch traced here: 73.6 us
  Pallas kernels  70.1 us (95%)
  local copies, waits for them, and re-layouts  2.74 us (4%)
    pallas_call x1, Pallas kernels, scatter(): pl.pallas_call(scatter_kernel, out_shape=jax.ShapeDtypeStruct((3, 2048),...  31.4 us
    pallas_call x1, Pallas kernels, gather(): pl.pallas_call(gather_kernel, out_shape=(jax.ShapeDtypeStruct((32, 4, 204...  21.7 us
    pallas_call x1, Pallas kernels, forces_of(): pl.pallas_call(force_kernel, out_shape=(jax.ShapeDtypeStruct((32, 48, TIL...  17 us
    unnamed x9, local copies, waits for them, and re-layouts  2.74 us

profile of v2, /device:TPU:18, one launch (start us, length us, event | category | flops | bytes accessed | tf_op | source)
XLA Modules:
  0.0 73.6 jit_solution(5724770813813884631)
XLA Ops:
  0.7 0.0 copy-start
  0.7 0.7 %copy-done = f32[3,2048]{1,0:T(4,128)S(1)} copy-done((f32[3,2048]{1,0:T(4,128)S(1)}, f32[3,2048]{1,0:T(4,128)}, u32[]{:S(2)}) %copy-start) | copy-done | bytes 24600
  1.4 0.0 copy-start.1
  1.4 0.7 copy-done.1
  2.1 0.0 copy-start.3
  2.1 21.7 %gather_atoms.1 = (f32[32,4,2048]{2,1,0:T(4,128)S(1)}, f32[8,4,2048]{2,1,0:T(4,128)S(1)}) custom-call(f32[3,2048]{1,0:T(4,128)S(1)} %copy-done, s32[16,128]{1,0:T(8,128)S(1)} %bitcast.4), custom_call_target="tpu_custom_call" | custom-call | tf_op jit(solution)/shard_map/gather_atoms/pallas_call | solution.py:368
  23.9 0.0 copy-start.2
  23.9 0.0 copy-done.3
  23.9 0.7 copy-done.2
  24.5 17.0 %pair_forces.1 = (f32[32,48,128]{2,1,0:T(8,128)S(1)}, f32[8,48,128]{2,1,0:T(8,128)S(1)}) custom-call(s32[1,1]{1,0:T(1,128)S(6)} %copy.7.count_ref, s32[2,384]{1,0:T(2,128)S(1)} %bitcast.5, f32[2,16]{1,0:T(2,128)S(1)} %copy-done.3, f32[32,4,2048]{2,1,0:T(4,128)S(1)} %get-tuple-element.9.row_ref, f32[8,4,2048]{2,1,0:T(4,128)S(1)} %get-tuple-element.10.col_ref), custom_call_target="tpu_custom_call" | custom-call | tf_op jit(solution)/shard_map/pair_forces/pallas_call | solution.py:198
  41.5 31.4 %scatter_forces.1 = f32[3,2048]{1,0:T(4,128)S(1)} custom-call(f32[32,48,128]{2,1,0:T(8,128)S(1)} %get-tuple-element.11.row_ref, f32[8,48,128]{2,1,0:T(8,128)S(1)} %get-tuple-element.12.col_ref), custom_call_target="tpu_custom_call" | custom-call | tf_op jit(solution)/shard_map/scatter_forces/pallas_call | solution.py:470
  73.0 0.6 copy.8
Async XLA Ops:
  0.7 0.8 %copy-start = (f32[3,2048]{1,0:T(4,128)S(1)}, f32[3,2048]{1,0:T(4,128)}, u32[]{:S(2)}) copy-start(f32[3,2048]{1,0:T(4,128)} %pos_ref.1) | copy-start | bytes 73732
  1.4 0.7 copy-start.1
  2.1 21.8 %copy-start.3 = (f32[2,16]{1,0:T(2,128)S(1)}, f32[2,16]{1,0:T(2,128)}, u32[]{:S(2)}) copy-start(f32[2,16]{1,0:T(2,128)} %params_ref.1) | copy-start | bytes 388
  23.9 0.7 copy-start.2

commit v3 on v2

v3 whole, which is shorter than its diff:
```python
import math

import jax
import jax.numpy as jnp
from jax import lax
from jax.experimental import pallas as pl
from jax.experimental.pallas import tpu as pltpu
from jax.sharding import PartitionSpec as P

TILE = 128
NTYPES = 16
CUTOFF_SQ = 6.25
LOG2E = math.log2(math.e)
KAPPA = 2.0 / (CUTOFF_SQ * LOG2E)
UNROLL = 16
ROW_TILES = 512
COL_TILES = 128
F32 = jnp.float32
BF16 = jnp.bfloat16
MESH = pl.DeviceIdType.MESH


def pieces(value):
    high = value.astype(BF16).astype(F32)
    rest = value - high
    middle = rest.astype(BF16).astype(F32)
    return high, middle, rest, rest - middle


def distance_stack(value, order):
    high, middle, _, low = pieces(value)
    part = {"h": high, "m": middle, "l": low}
    return [jnp.concatenate([part[order[k]], part[order[k + 1]]], axis=0).astype(BF16) for k in (0, 2, 4)]


def moment_stack(value, upper):
    high, _, rest, low = pieces(value)
    return jnp.concatenate([jnp.where(upper, high, rest), jnp.where(upper, low, 0.0)], axis=0).astype(BF16)


def lanes_of(kinds):
    eye = lax.broadcasted_iota(jnp.int32, (NTYPES, NTYPES), 0) == lax.broadcasted_iota(jnp.int32, (NTYPES, NTYPES), 1)
    return jnp.sum(jnp.where(eye, kinds, 0.0), axis=1, keepdims=True)


def type_reader(params_ref):
    subf = lax.broadcasted_iota(jnp.int32, (8, TILE), 0).astype(F32)
    root = lanes_of(jnp.sqrt(params_ref[0:1, :]))
    root_a = jnp.broadcast_to(root[0:8], (8, TILE))
    root_b = jnp.broadcast_to(root[8:16], (8, TILE))

    def typed(kind):
        hit_a = subf == kind
        hit_b = subf + 8.0 == kind
        onehot = jnp.concatenate([jnp.where(hit_a, 1.0, 0.0), jnp.where(hit_b, 1.0, 0.0)], axis=0).astype(BF16)
        depth = jnp.sum(jnp.where(hit_a, root_a, 0.0) + jnp.where(hit_b, root_b, 0.0), axis=0, keepdims=True)
        return onehot, jnp.broadcast_to(depth, (8, TILE))

    return typed


def wide(ref, dev, comp, lane):
    return jnp.broadcast_to(ref[dev, comp : comp + 1, pl.ds(lane, TILE)], (8, TILE))


def spread(quad, x, y, z, last):
    return jnp.where(quad == 0, x, jnp.where(quad == 1, y, jnp.where(quad == 2, z, last)))


def column_preparer(params_ref, col_ref, feat, mom, cen, vel):
    sub = lax.broadcasted_iota(jnp.int32, (8, TILE), 0)
    quad = sub & 3
    width = params_ref[1:2, :]
    total = 0.5 * (lanes_of(width) + width)
    t_high, t_mid, _, t_low = pieces((CUTOFF_SQ * LOG2E) / (total * total))
    table48 = jnp.concatenate([t_high, t_mid, t_low], axis=0).astype(BF16)
    typed = type_reader(params_ref)
    zero_pack = jnp.zeros((16, TILE), BF16)

    def prepare(dev, k):
        b = dev * 16 + k
        x, y, z, kind = (wide(col_ref, dev, c, k * TILE) for c in range(4))
        here = spread(quad, x, y, z, 0.0)
        centre = jnp.sum(here, axis=1, keepdims=True) * (1.0 / TILE)
        cen[b] = jnp.broadcast_to(centre, (8, TILE))
        v = here - centre
        norm = jnp.sum(jnp.where(sub < 3, v * v, 0.0), axis=0, keepdims=True)
        onehot, depth = typed(kind)
        z8 = jnp.where(sub < 3, v * (2.0 / CUTOFF_SQ), jnp.where(sub == 3, 1.0, jnp.where(sub == 4, norm * (-1.0 / CUTOFF_SQ), 0.0)))
        second = jnp.dot(table48, onehot, preferred_element_type=F32).astype(BF16)
        stack = jnp.concatenate(distance_stack(z8, "hmlhmh") + [second, zero_pack, zero_pack], axis=0)
        feat[b] = stack.T
        mom[b] = moment_stack(jnp.where(quad == 3, 1.0, v) * depth, sub < 4)
        vel[b] = jnp.where(sub == 3, depth * KAPPA, v)

    def shard(dev):
        for k in range(16):
            prepare(dev, k)

    return shard


def force_kernel(count_ref, tiles_hbm, row_ref, feat, mom, cen, vel, params_ref, row_out, col_out, acc_row, acc_col, slope, mine, offset, scale, tiles_ref, load_sem):
    load_tiles = pltpu.make_async_copy(tiles_hbm, tiles_ref, load_sem)
    load_tiles.start()
    sub = lax.broadcasted_iota(jnp.int32, (8, TILE), 0)
    quad = sub & 3
    upper = sub < 4
    unit = jnp.where(sub == 4, 1.0, 0.0)
    typed = type_reader(params_ref)
    zero_pack = jnp.zeros((16, TILE), BF16)
    acc_row[...] = jnp.zeros_like(acc_row)
    acc_col[...] = jnp.zeros_like(acc_col)
    slope[...] = jnp.zeros_like(slope)
    mine[...] = jnp.zeros_like(mine)
    offset[...] = jnp.zeros_like(offset)
    scale[...] = jnp.zeros_like(scale)
    load_tiles.wait()
    count = count_ref[0, 0]

    def fold(out):
        first = out[0:8]
        return first + pltpu.roll(first, 4, 0) + out[8:16]

    zeros3 = [zero_pack] * 3
    zeros2 = [zero_pack] * 2

    def names(slot):
        live = (slot >= 0) & (slot < count)
        at = jnp.clip(slot, 0, count - 1)
        return live, tiles_ref[0, at], tiles_ref[1, at]

    def spread_out(slot, k):
        _, a, b = names(slot)
        owner = a // 16
        dev = (owner & 1) * 16 + (owner >> 1)
        lane = pl.multiple_of((a & 15) * TILE, TILE)
        x, y, z = (wide(row_ref, dev, c, lane) - jnp.broadcast_to(cen[b, c : c + 1, :], (8, TILE)) for c in range(3))
        kind = wide(row_ref, dev, 3, lane)
        onehot, depth = typed(kind)
        q = 1.0 - (x * x + y * y + z * z) * (1.0 / CUTOFF_SQ)
        xz = spread(quad, x, y, z, 1.0)
        z8 = jnp.where(sub < 3, xz, jnp.where(sub == 3, q, unit))
        near = jnp.concatenate(distance_stack(z8, "hhhmml") + zeros3 + zeros2, axis=0)
        kinds = jnp.concatenate(zeros3 + [onehot] * 3 + zeros2, axis=0)
        both = jnp.dot(feat[b], jnp.concatenate([near, kinds], axis=1), preferred_element_type=F32)
        c = jnp.maximum(both[:, :TILE], 0.0)
        decay = both[:, TILE:]
        u = c * decay
        g = (c * (u + 2.0 * LOG2E)) * jnp.exp2(u - decay)
        g_high = g.astype(BF16)
        g_low = (g - g_high.astype(F32)).astype(BF16)
        slope[k, 0:TILE, :] = g_high
        slope[k, TILE : 2 * TILE, :] = g_low
        mine[k] = moment_stack(xz * depth, upper)
        offset[k] = xz
        scale[k] = depth * KAPPA

    def gather_in(slot, k):
        live, a, b = names(slot)
        a_to = pl.multiple_of(jnp.where(live, a, ROW_TILES) * 8, 8)
        b_to = pl.multiple_of(jnp.where(live, b, COL_TILES) * 8, 8)
        sides = jnp.concatenate([mom[b], mine[k]], axis=0)
        g = slope[k]
        across = jnp.concatenate([g[:TILE].T, g[TILE:].T], axis=0)
        out = jnp.dot(
            jnp.concatenate([sides, sides], axis=1),
            jnp.concatenate([g, across], axis=1),
            preferred_element_type=F32,
        )
        to_i = fold(out[0:16, :TILE])
        to_j = fold(out[16:32, TILE:])
        weight = jnp.broadcast_to(to_i[3:4], (8, TILE))
        on_i = (offset[k] * weight - to_i) * scale[k]
        return a_to, b_to, on_i, to_j

    @pl.loop(0, pl.cdiv(count, UNROLL) + 1)
    def _(step):
        done = [gather_in((step - 1) * UNROLL + k, k) for k in range(UNROLL)]
        for k in range(UNROLL):
            spread_out(step * UNROLL + k, k)
        for a_to, b_to, on_i, to_j in done:
            acc_row[pl.ds(a_to, 8), :] += on_i
            acc_col[pl.ds(b_to, 8), :] += to_j

    @pl.loop(0, COL_TILES, step=4)
    def _(b0):
        for k in range(4):
            b = b0 + k
            at = pl.multiple_of(b * 8, 8)
            got = acc_col[pl.ds(at, 8), :]
            v = vel[b]
            weight = jnp.broadcast_to(got[3:4], (8, TILE))
            depth = jnp.broadcast_to(v[3:4], (8, TILE))
            acc_col[pl.ds(at, 8), :] = (v * weight - got) * depth

    for q in range(32):
        slot = (q & 1) * 16 + (q >> 1)
        for c in range(3):
            row_out[slot, c * 16 : c * 16 + 16, :] = acc_row[pl.ds(q * 128 + c, 16, stride=8), :]
    for p in range(8):
        for c in range(3):
            col_out[p, c * 16 : c * 16 + 16, :] = acc_col[pl.ds(p * 128 + c, 16, stride=8), :]


def forces_of(count, tiles, row_data, *columns):
    hbm = pl.BlockSpec(memory_space=pltpu.HBM)
    vmem = pl.BlockSpec(memory_space=pltpu.VMEM)
    return pl.pallas_call(
        force_kernel,
        out_shape=(jax.ShapeDtypeStruct((32, 48, TILE), F32), jax.ShapeDtypeStruct((8, 48, TILE), F32)),
        in_specs=[pl.BlockSpec(memory_space=pltpu.SMEM), hbm] + [vmem] * 6,
        out_specs=(vmem, vmem),
        scratch_shapes=[
            pltpu.VMEM(((ROW_TILES + 1) * 8, TILE), F32),
            pltpu.VMEM(((COL_TILES + 1) * 8, TILE), F32),
            pltpu.VMEM((UNROLL, 2 * TILE, TILE), BF16),
            pltpu.VMEM((UNROLL, 16, TILE), BF16),
            pltpu.VMEM((UNROLL, 8, TILE), F32),
            pltpu.VMEM((UNROLL, 8, TILE), F32),
            pltpu.SMEM((2, 384), jnp.int32),
            pltpu.SemaphoreType.DMA,
        ],
        compiler_params=pltpu.CompilerParams(vmem_limit_bytes=40 * 1024 * 1024),
        name="pair_forces",
    )(count, tiles, row_data, *columns)


def ring(v, d):
    return (v + d + 4) % 4


def place():
    p, q = lax.axis_index("row"), lax.axis_index("col")
    return p // 2, p % 2, q // 8, (q // 2) % 4, q % 2


def device(y, zl, zh, x, core):
    return (y * 2 + zl, zh * 8 + x * 2 + core)


STEPS = {"far": 2, "up": 1, "down": -1}


def neighbours(y, zl, zh, x, core):
    near = {"twin": device(y, zl, zh, x, 1 - core), "pal": device(y, 1 - zl, zh, x, core)}
    for name, d in STEPS.items():
        near["z_" + name] = device(y, zl, ring(zh, d), x, core)
        near["x_" + name] = device(y, zl, zh, ring(x, d), core)
        near["y_" + name] = device(ring(y, d), zl, zh, x, core)
    return near


def greet(near):
    barrier = pltpu.get_barrier_semaphore()
    for target in near.values():
        pl.semaphore_signal(barrier, inc=1, device_id=target, device_id_type=MESH)
    pl.semaphore_wait(barrier, len(near))


class Copies:
    def __init__(self, near, send_sem, recv_sem):
        self.near, self.send_sem, self.recv_sem = near, send_sem, recv_sem
        self.started = []

    def start(self, source, target, to):
        k = len(self.started)
        copy = pltpu.make_async_remote_copy(
            src_ref=source,
            dst_ref=target,
            send_sem=self.send_sem.at[k],
            recv_sem=self.recv_sem.at[k],
            device_id=self.near[to],
            device_id_type=MESH,
        )
        copy.start()
        self.started.append(copy)
        return copy

    def finish(self):
        for copy in self.started:
            copy.wait_send()


GATHER_COPIES = 38
SCATTER_COPIES = 23


def gather_kernel(pos_hbm, type_hbm, params_hbm, row_ref, col_ref, feat, mom, cen, vel, params_ref, pos_in, type_in, load_sem, send_sem, recv_sem):
    load_pos = pltpu.make_async_copy(pos_hbm, pos_in, load_sem.at[0])
    load_type = pltpu.make_async_copy(type_hbm, type_in, load_sem.at[1])
    load_params = pltpu.make_async_copy(params_hbm, params_ref, load_sem.at[2])
    load_pos.start()
    load_type.start()
    load_params.start()
    y, zl, zh, x, core = place()
    near = neighbours(y, zl, zh, x, core)
    at = lambda xx, zz: core * 16 + zz * 4 + xx
    col_at = lambda yy, ll: yy * 2 + ll
    mine, col_mine, col_pal = at(x, zh), col_at(y, zl), col_at(y, 1 - zl)
    load_pos.wait()
    load_type.wait()
    for ref, slot in ((row_ref, mine), (col_ref, col_mine)):
        ref[slot, 0:3, :] = pos_in[...]
        for k in range(16):
            ref[slot, 3:4, k * TILE : (k + 1) * TILE] = type_in[k : k + 1, :].astype(F32)
    greet(near)
    net = Copies(near, send_sem, recv_sem)

    def send(ref, slot, to):
        return net.start(ref.at[slot], ref.at[slot], to)

    along_z = {name: send(row_ref, mine, "z_" + name) for name in STEPS}
    along_x, along_y, twins = {}, {}, []
    pal = send(col_ref, col_mine, "pal")

    def pass_on(zz, key):
        along_x[key] = {name: send(row_ref, at(x, zz), "x_" + name) for name in STEPS}
        twins.append(send(row_ref, at(x, zz), "twin"))

    def pass_col(slot, key):
        along_y[key] = {name: send(col_ref, slot, "y_" + name) for name in STEPS}

    def hand_over(zz, key):
        for name in ("up", "down", "far"):
            along_x[key][name].wait_recv()
            twins.append(send(row_ref, at(ring(x, -STEPS[name]), zz), "twin"))

    pass_on(zh, "own")
    pass_col(col_mine, 0)
    load_params.wait()
    prepare = column_preparer(params_ref, col_ref, feat, mom, cen, vel)
    prepare(col_mine)
    pal.wait_recv()
    pass_col(col_pal, 1)
    for name in ("up", "down"):
        along_z[name].wait_recv()
        pass_on(ring(zh, -STEPS[name]), name)
    prepare(col_pal)
    hand_over(zh, "own")
    along_z["far"].wait_recv()
    pass_on(ring(zh, 2), "far")
    for name in ("up", "down"):
        along_y[0][name].wait_recv()
        prepare(col_at(ring(y, -STEPS[name]), zl))
    hand_over(ring(zh, -1), "up")
    hand_over(ring(zh, 1), "down")
    for name in ("up", "down"):
        along_y[1][name].wait_recv()
        prepare(col_at(ring(y, -STEPS[name]), 1 - zl))
    hand_over(ring(zh, 2), "far")
    for key, ll in ((0, zl), (1, 1 - zl)):
        along_y[key]["far"].wait_recv()
        prepare(col_at(ring(y, 2), ll))
    for copy in twins:
        copy.wait_recv()
    net.finish()


def in_hbm(array):
    return pltpu.with_memory_space_constraint(array, pltpu.HBM)


def gather(positions, kinds, params):
    hbm = pl.BlockSpec(memory_space=pltpu.HBM)
    vmem = pl.BlockSpec(memory_space=pltpu.VMEM)
    out = lambda *shape: jax.ShapeDtypeStruct(shape, F32)
    row_data, _, *columns = pl.pallas_call(
        gather_kernel,
        out_shape=(
            out(32, 4, 2048),
            out(8, 4, 2048),
            jax.ShapeDtypeStruct((COL_TILES, TILE, TILE), BF16),
            jax.ShapeDtypeStruct((COL_TILES, 16, TILE), BF16),
            out(COL_TILES, 8, TILE),
            out(COL_TILES, 8, TILE),
            out(2, NTYPES),
        ),
        in_specs=[hbm] * 3,
        out_specs=(vmem,) * 7,
        scratch_shapes=[
            pltpu.VMEM((3, 2048), F32),
            pltpu.VMEM((16, TILE), jnp.int32),
            pltpu.SemaphoreType.DMA((3,)),
            pltpu.SemaphoreType.DMA((GATHER_COPIES,)),
            pltpu.SemaphoreType.DMA((GATHER_COPIES,)),
        ],
        compiler_params=pltpu.CompilerParams(
            collective_id=0, has_side_effects=True, vmem_limit_bytes=24 * 1024 * 1024
        ),
        name="gather_atoms",
    )(*map(in_hbm, (positions, kinds, params)))
    return row_data, columns


def scatter_kernel(row_ref, col_ref, out_ref, from_twin, row_sum, x_in, z_out, z_in, y_in, col_sum, pal_in, send_sem, recv_sem):
    y, zl, zh, x, core = place()
    near = neighbours(y, zl, zh, x, core)
    greet(near)
    net = Copies(near, send_sem, recv_sem)
    offsets = (2, 1, -1, 0)
    order = ("far", "up", "down")

    twins = []
    for d in offsets:
        rows = ring(zh, d) * 4
        twins.append(net.start(row_ref.at[pl.ds((1 - core) * 16 + rows, 4)], from_twin.at[pl.ds(rows, 4)], "twin"))
    along_y = [net.start(col_ref.at[pl.ds(ring(y, STEPS[n]) * 2, 2)], y_in.at[k], "y_" + n) for k, n in enumerate(order)]

    along_x = []
    for i, d in enumerate(offsets):
        rows = ring(zh, d) * 4
        twins[i].wait_recv()
        row_sum[pl.ds(rows, 4)] = row_ref[pl.ds(core * 16 + rows, 4)] + from_twin[pl.ds(rows, 4)]
        along_x.append(
            [net.start(row_sum.at[rows + ring(x, STEPS[n])], x_in.at[i, k], "x_" + n) for k, n in enumerate(order)]
        )

    for copy in along_y:
        copy.wait_recv()
    here = y * 2
    col_sum[0] = col_ref[here + 1 - zl] + y_in[0, 1 - zl] + y_in[1, 1 - zl] + y_in[2, 1 - zl]
    pal = net.start(col_sum.at[0], pal_in, "pal")
    col_sum[1] = col_ref[here + zl] + y_in[0, zl] + y_in[1, zl] + y_in[2, zl]

    along_z = []
    for i, d in enumerate(offsets):
        for copy in along_x[i]:
            copy.wait_recv()
        total = row_sum[ring(zh, d) * 4 + x] + x_in[i, 0] + x_in[i, 1] + x_in[i, 2]
        if d:
            z_out[i] = total
            along_z.append(net.start(z_out.at[i], z_in.at[i], "z_" + order[i]))
        else:
            col_sum[1] = col_sum[1] + total
    pal.wait_recv()
    col_sum[1] = col_sum[1] + pal_in[...]
    for copy in along_z:
        copy.wait_recv()
    col_sum[1] = col_sum[1] + (z_in[0] + z_in[1] + z_in[2])
    for c in range(3):
        for k in range(16):
            out_ref[c : c + 1, k * TILE : (k + 1) * TILE] = col_sum[1, c * 16 + k : c * 16 + k + 1, :]
    net.finish()


def scatter(row_part, col_part):
    vmem = pl.BlockSpec(memory_space=pltpu.VMEM)
    block = lambda *n: pltpu.VMEM((*n, 48, TILE), F32)
    return pl.pallas_call(
        scatter_kernel,
        out_shape=jax.ShapeDtypeStruct((3, 2048), F32),
        in_specs=[vmem, vmem],
        out_specs=vmem,
        scratch_shapes=[
            block(16),
            block(16),
            block(4, 3),
            block(3),
            block(3),
            block(3, 2),
            block(2),
            block(),
            pltpu.SemaphoreType.DMA((SCATTER_COPIES,)),
            pltpu.SemaphoreType.DMA((SCATTER_COPIES,)),
        ],
        compiler_params=pltpu.CompilerParams(
            collective_id=1, has_side_effects=True, vmem_limit_bytes=16 * 1024 * 1024
        ),
        name="scatter_forces",
    )(row_part, col_part)


def shards(positions, type_ids, type_params, pair_tiles, pair_counts):
    row_data, columns = gather(positions, type_ids.reshape(16, TILE), type_params)
    tiles = pair_tiles[0, 0].T
    row_part, col_part = forces_of(pair_counts, in_hbm(tiles), row_data, *columns)
    return scatter(row_part, col_part)


def solution(mesh):
    placed = (
        P(None, ("row", "col")),
        P(("row", "col")),
        P(),
        P("row", "col", None, None),
        P("row", "col"),
    )
    return jax.shard_map(
        shards, mesh=mesh, in_specs=placed, out_specs=P(None, ("row", "col")), check_vma=False
    )
```

time: 73.8 us -> 63.9 us (0.87)
  the two profiles are of different devices: /device:TPU:18 before, /device:TPU:1 now
where the time goes in v3:
time: 63.9 us; the launch traced here: 63.8 us
  Pallas kernels  62.5 us (98%)
  between operations  0.68 us (1%)
    pallas_call x1, Pallas kernels, forces_of(): pl.pallas_call(force_kernel, out_shape=(jax.ShapeDtypeStruct((32, 48, TIL...  25.7 us
    pallas_call x1, Pallas kernels, gather(): pl.pallas_call(gather_kernel, out_shape=(out(32, 4, 2048), out(8, 4, 2048...  24.1 us
    pallas_call x1, Pallas kernels, scatter(): pl.pallas_call(scatter_kernel, out_shape=jax.ShapeDtypeStruct((3, 2048),...  12.8 us

profile of v3, /device:TPU:1, one launch (start us, length us, event | category | flops | bytes accessed | tf_op | source)
XLA Modules:
  0.0 63.8 jit_solution(11040308654031231385)
XLA Ops:
  0.7 24.1 %gather_atoms.1 = (f32[32,4,2048]{2,1,0:T(4,128)S(1)}, f32[8,4,2048]{2,1,0:T(4,128)}, bf16[128,128,128]{2,1,0:T(8,128)(2,1)S(1)}, bf16[128,16,128]{2,1,0:T(8,128...) custom-call(f32[3,2048]{1,0:T(4,128)} %pos_hbm.1, s32[16,128]{1,0:T(8,128)} %bitcast.4, ...), custom_call_target="tpu_custom_call" | custom-call | tf_op jit(solution)/shard_map/gather_atoms/pallas_call | solution.py:368
  24.7 25.7 %pair_forces.1 = (f32[32,48,128]{2,1,0:T(8,128)S(1)}, f32[8,48,128]{2,1,0:T(8,128)S(1)}) custom-call(s32[1,1]{1,0:T(1,128)S(6)} %copy.7.count_ref, s32[2,384]{1,0:T(2,128)} %bitcast.5, f32[32,4,2048]{2,1,0:T(4,128)S(1)} %get-tuple-element.13.row_ref, bf16[128,128,128]{2,1,0:T(8,128)(2,1)S(1)} %get-tuple-element.14.feat, ...), custom_call_target="tpu_custom_call" | custom-call | tf_op jit(solution)/shard_map/pair_forces/pallas_call | solution.py:209
  50.4 12.8 %scatter_forces.1 = f32[3,2048]{1,0:T(4,128)S(1)} custom-call(f32[32,48,128]{2,1,0:T(8,128)S(1)} %get-tuple-element.19.row_ref, f32[8,48,128]{2,1,0:T(8,128)S(1)} %get-tuple-element.20.col_ref), custom_call_target="tpu_custom_call" | custom-call | tf_op jit(solution)/shard_map/scatter_forces/pallas_call | solution.py:450
  63.1 0.6 copy.8

commit v4 on v3

--- a/solution.py
+++ b/solution.py
@@ -12,7 +12,13 @@
 CUTOFF_SQ = 6.25
 LOG2E = math.log2(math.e)
 KAPPA = 2.0 / (CUTOFF_SQ * LOG2E)
-UNROLL = 16
+WIDTH_SCALE = 0.5 / math.sqrt(CUTOFF_SQ * LOG2E)
+GROUP = 8
+TURNS = 4
+UNROLL = GROUP * TURNS
+G2 = 2 * GROUP
+U2 = GROUP
+FIRST = 128
 ROW_TILES = 512
 COL_TILES = 128
 F32 = jnp.float32
@@ -34,29 +40,13 @@
 
 
 def moment_stack(value, upper):
-    high, _, rest, low = pieces(value)
-    return jnp.concatenate([jnp.where(upper, high, rest), jnp.where(upper, low, 0.0)], axis=0).astype(BF16)
-
-
-def lanes_of(kinds):
-    eye = lax.broadcasted_iota(jnp.int32, (NTYPES, NTYPES), 0) == lax.broadcasted_iota(jnp.int32, (NTYPES, NTYPES), 1)
-    return jnp.sum(jnp.where(eye, kinds, 0.0), axis=1, keepdims=True)
-
-
-def type_reader(params_ref):
-    subf = lax.broadcasted_iota(jnp.int32, (8, TILE), 0).astype(F32)
-    root = lanes_of(jnp.sqrt(params_ref[0:1, :]))
-    root_a = jnp.broadcast_to(root[0:8], (8, TILE))
-    root_b = jnp.broadcast_to(root[8:16], (8, TILE))
-
-    def typed(kind):
-        hit_a = subf == kind
-        hit_b = subf + 8.0 == kind
-        onehot = jnp.concatenate([jnp.where(hit_a, 1.0, 0.0), jnp.where(hit_b, 1.0, 0.0)], axis=0).astype(BF16)
-        depth = jnp.sum(jnp.where(hit_a, root_a, 0.0) + jnp.where(hit_b, root_b, 0.0), axis=0, keepdims=True)
-        return onehot, jnp.broadcast_to(depth, (8, TILE))
-
-    return typed
+    high = value.astype(BF16).astype(F32)
+    return jnp.where(upper, high, value - high)
+
+
+def look_up(table, kind):
+    both = jnp.take_along_axis(table, kind.astype(jnp.int32), axis=1)
+    return jnp.broadcast_to(both[0:1], (8, TILE)), jnp.broadcast_to(both[4:5], (8, TILE))
 
 
 def wide(ref, dev, comp, lane):
@@ -67,15 +57,14 @@
     return jnp.where(quad == 0, x, jnp.where(quad == 1, y, jnp.where(quad == 2, z, last)))
 
 
-def column_preparer(params_ref, col_ref, feat, mom, cen, vel):
+def column_preparer(table, col_ref, feat, mom, cen, vel, wid):
     sub = lax.broadcasted_iota(jnp.int32, (8, TILE), 0)
     quad = sub & 3
-    width = params_ref[1:2, :]
-    total = 0.5 * (lanes_of(width) + width)
-    t_high, t_mid, _, t_low = pieces((CUTOFF_SQ * LOG2E) / (total * total))
-    table48 = jnp.concatenate([t_high, t_mid, t_low], axis=0).astype(BF16)
-    typed = type_reader(params_ref)
-    zero_pack = jnp.zeros((16, TILE), BF16)
+    zero8 = jnp.zeros((8, TILE), F32)
+    types = table[...]
+    zeros = jnp.zeros((64, TILE), BF16)
+    row = lax.broadcasted_iota(jnp.int32, (TILE, TILE), 0)
+    pick = jnp.where((row >= 48) & (row < 51), 1.0, 0.0).astype(BF16)
 
     def prepare(dev, k):
         b = dev * 16 + k
@@ -85,11 +74,14 @@
         cen[b] = jnp.broadcast_to(centre, (8, TILE))
         v = here - centre
         norm = jnp.sum(jnp.where(sub < 3, v * v, 0.0), axis=0, keepdims=True)
-        onehot, depth = typed(kind)
+        depth, width = look_up(types, kind)
         z8 = jnp.where(sub < 3, v * (2.0 / CUTOFF_SQ), jnp.where(sub == 3, 1.0, jnp.where(sub == 4, norm * (-1.0 / CUTOFF_SQ), 0.0)))
-        second = jnp.dot(table48, onehot, preferred_element_type=F32).astype(BF16)
-        stack = jnp.concatenate(distance_stack(z8, "hmlhmh") + [second, zero_pack, zero_pack], axis=0)
-        feat[b] = stack.T
+        high, middle, _, low = pieces(width)
+        widths = jnp.where(sub == 0, high, jnp.where(sub == 1, middle, jnp.where(sub == 2, low, 0.0)))
+        widths = jnp.concatenate([widths, zero8], axis=0).astype(BF16)
+        turned = jnp.concatenate(distance_stack(z8, "hmlhmh") + [widths, zeros], axis=0).T
+        feat[b] = turned
+        wid[b] = jnp.dot(turned, pick, preferred_element_type=F32)
         mom[b] = moment_stack(jnp.where(quad == 3, 1.0, v) * depth, sub < 4)
         vel[b] = jnp.where(sub == 3, depth * KAPPA, v)
 
@@ -100,88 +92,98 @@
     return shard
 
 
-def force_kernel(count_ref, tiles_hbm, row_ref, feat, mom, cen, vel, params_ref, row_out, col_out, acc_row, acc_col, slope, mine, offset, scale, tiles_ref, load_sem):
-    load_tiles = pltpu.make_async_copy(tiles_hbm, tiles_ref, load_sem)
+def force_kernel(count_ref, tiles_hbm, row_ref, feat, mom, cen, vel, wid, table, row_out, col_out, acc_row, acc_col, slope, mine, offset, scale, span, reach, tiles_ref, load_sem):
+    load_tiles = pltpu.make_async_copy(tiles_hbm, tiles_ref.at[:, pl.ds(FIRST, 384)], load_sem)
     load_tiles.start()
     sub = lax.broadcasted_iota(jnp.int32, (8, TILE), 0)
     quad = sub & 3
     upper = sub < 4
     unit = jnp.where(sub == 4, 1.0, 0.0)
-    typed = type_reader(params_ref)
-    zero_pack = jnp.zeros((16, TILE), BF16)
+    types = table[...]
+    zeros80 = jnp.zeros((80, TILE), BF16)
+    zeros128 = jnp.zeros((TILE, TILE), BF16)
     acc_row[...] = jnp.zeros_like(acc_row)
     acc_col[...] = jnp.zeros_like(acc_col)
-    slope[...] = jnp.zeros_like(slope)
-    mine[...] = jnp.zeros_like(mine)
-    offset[...] = jnp.zeros_like(offset)
-    scale[...] = jnp.zeros_like(scale)
     load_tiles.wait()
     count = count_ref[0, 0]
+    for k in range(-2 * GROUP, 6 * GROUP):
+        at = FIRST + k + (0 if k < 0 else count)
+        tiles_ref[0, at] = ROW_TILES
+        tiles_ref[1, at] = COL_TILES
 
     def fold(out):
-        first = out[0:8]
-        return first + pltpu.roll(first, 4, 0) + out[8:16]
-
-    zeros3 = [zero_pack] * 3
-    zeros2 = [zero_pack] * 2
-
-    def names(slot):
-        live = (slot >= 0) & (slot < count)
-        at = jnp.clip(slot, 0, count - 1)
-        return live, tiles_ref[0, at], tiles_ref[1, at]
-
-    def spread_out(slot, k):
-        _, a, b = names(slot)
-        owner = a // 16
-        dev = (owner & 1) * 16 + (owner >> 1)
+        return out + pltpu.roll(out, 4, 0)
+
+    def nearness(slot, k):
+        a, b = tiles_ref[0, slot] & (ROW_TILES - 1), tiles_ref[1, slot] & (COL_TILES - 1)
+        dev = (a & 16) + (a >> 5)
         lane = pl.multiple_of((a & 15) * TILE, TILE)
         x, y, z = (wide(row_ref, dev, c, lane) - jnp.broadcast_to(cen[b, c : c + 1, :], (8, TILE)) for c in range(3))
         kind = wide(row_ref, dev, 3, lane)
-        onehot, depth = typed(kind)
+        depth, width = look_up(types, kind)
         q = 1.0 - (x * x + y * y + z * z) * (1.0 / CUTOFF_SQ)
         xz = spread(quad, x, y, z, 1.0)
         z8 = jnp.where(sub < 3, xz, jnp.where(sub == 3, q, unit))
-        near = jnp.concatenate(distance_stack(z8, "hhhmml") + zeros3 + zeros2, axis=0)
-        kinds = jnp.concatenate(zeros3 + [onehot] * 3 + zeros2, axis=0)
-        both = jnp.dot(feat[b], jnp.concatenate([near, kinds], axis=1), preferred_element_type=F32)
-        c = jnp.maximum(both[:, :TILE], 0.0)
-        decay = both[:, TILE:]
+        mine[k][...] = moment_stack(xz * depth, upper)
+        offset[k][...] = xz
+        scale[k][...] = depth * KAPPA
+        span[k][...] = width
+        return b, jnp.concatenate(distance_stack(z8, "hhhmml") + [zeros80], axis=0)
+
+    def measure(slot, k):
+        sides = [nearness(slot + n, k + n) for n in range(2)]
+        feats = jnp.concatenate([feat[b] for b, _ in sides], axis=1)
+        first, second = (near for _, near in sides)
+        weights = jnp.concatenate(
+            [jnp.concatenate([first, zeros128], axis=1), jnp.concatenate([zeros128, second], axis=1)], axis=0
+        )
+        reach[k // 2 % U2][...] = jnp.dot(feats, weights, preferred_element_type=F32)
+
+    def spread_out(slot, k):
+        b = tiles_ref[1, slot] & (COL_TILES - 1)
+        half = (k % 2) * TILE
+        c = jnp.maximum(reach[k // 2 % U2][:, half : half + TILE], 0.0)
+        spans = wid[b].reshape(16, 8, TILE) + span[k][...][None]
+        inverse = pl.reciprocal(spans.reshape(TILE, TILE), approx=True)
+        decay = inverse * inverse
         u = c * decay
         g = (c * (u + 2.0 * LOG2E)) * jnp.exp2(u - decay)
         g_high = g.astype(BF16)
         g_low = (g - g_high.astype(F32)).astype(BF16)
-        slope[k, 0:TILE, :] = g_high
-        slope[k, TILE : 2 * TILE, :] = g_low
-        mine[k] = moment_stack(xz * depth, upper)
-        offset[k] = xz
-        scale[k] = depth * KAPPA
+        slope[k % G2][0:TILE, :] = g_high
+        slope[k % G2][TILE : 2 * TILE, :] = g_low
 
     def gather_in(slot, k):
-        live, a, b = names(slot)
-        a_to = pl.multiple_of(jnp.where(live, a, ROW_TILES) * 8, 8)
-        b_to = pl.multiple_of(jnp.where(live, b, COL_TILES) * 8, 8)
-        sides = jnp.concatenate([mom[b], mine[k]], axis=0)
-        g = slope[k]
+        a, b = tiles_ref[0, slot], tiles_ref[1, slot]
+        a_to, b_to = pl.multiple_of(a * 8, 8), pl.multiple_of(b * 8, 8)
+        sides = jnp.concatenate([mom[b & (COL_TILES - 1)], mine[k][...]], axis=0).astype(BF16)
+        g = slope[k % G2][...]
         across = jnp.concatenate([g[:TILE].T, g[TILE:].T], axis=0)
         out = jnp.dot(
             jnp.concatenate([sides, sides], axis=1),
             jnp.concatenate([g, across], axis=1),
             preferred_element_type=F32,
         )
-        to_i = fold(out[0:16, :TILE])
-        to_j = fold(out[16:32, TILE:])
+        to_i = fold(out[0:8, :TILE])
+        to_j = fold(out[8:16, TILE:])
         weight = jnp.broadcast_to(to_i[3:4], (8, TILE))
-        on_i = (offset[k] * weight - to_i) * scale[k]
+        on_i = (offset[k][...] * weight - to_i) * scale[k][...]
         return a_to, b_to, on_i, to_j
 
-    @pl.loop(0, pl.cdiv(count, UNROLL) + 1)
-    def _(step):
-        done = [gather_in((step - 1) * UNROLL + k, k) for k in range(UNROLL)]
-        for k in range(UNROLL):
-            spread_out(step * UNROLL + k, k)
-        for a_to, b_to, on_i, to_j in done:
-            acc_row[pl.ds(a_to, 8), :] += on_i
-            acc_col[pl.ds(b_to, 8), :] += to_j
+    def collect(slot, k):
+        a_to, b_to, on_i, to_j = gather_in(slot, k)
+        acc_row[pl.ds(a_to, 8), :] += on_i
+        acc_col[pl.ds(b_to, 8), :] += to_j
+
+    @pl.loop(0, pl.cdiv(pl.cdiv(count, GROUP) + 2, TURNS))
+    def _(turn):
+        base = FIRST + turn * (TURNS * GROUP)
+        for h in range(TURNS):
+            for n in range(GROUP):
+                collect(base + (h - 2) * GROUP + n, (h - 2) % TURNS * GROUP + n)
+                spread_out(base + (h - 1) * GROUP + n, (h - 1) % TURNS * GROUP + n)
+                if n % 2:
+                    measure(base + h * GROUP + n - 1, h * GROUP + n - 1)
 
     @pl.loop(0, COL_TILES, step=4)
     def _(b0):
@@ -209,16 +211,18 @@
     return pl.pallas_call(
         force_kernel,
         out_shape=(jax.ShapeDtypeStruct((32, 48, TILE), F32), jax.ShapeDtypeStruct((8, 48, TILE), F32)),
-        in_specs=[pl.BlockSpec(memory_space=pltpu.SMEM), hbm] + [vmem] * 6,
+        in_specs=[pl.BlockSpec(memory_space=pltpu.SMEM), hbm] + [vmem] * 7,
         out_specs=(vmem, vmem),
         scratch_shapes=[
             pltpu.VMEM(((ROW_TILES + 1) * 8, TILE), F32),
             pltpu.VMEM(((COL_TILES + 1) * 8, TILE), F32),
-            pltpu.VMEM((UNROLL, 2 * TILE, TILE), BF16),
-            pltpu.VMEM((UNROLL, 16, TILE), BF16),
-            pltpu.VMEM((UNROLL, 8, TILE), F32),
-            pltpu.VMEM((UNROLL, 8, TILE), F32),
-            pltpu.SMEM((2, 384), jnp.int32),
+            [pltpu.VMEM((2 * TILE, TILE), BF16)] * G2,
+            [pltpu.VMEM((8, TILE), F32)] * UNROLL,
+            [pltpu.VMEM((8, TILE), F32)] * UNROLL,
+            [pltpu.VMEM((8, TILE), F32)] * UNROLL,
+            [pltpu.VMEM((8, TILE), F32)] * UNROLL,
+            [pltpu.VMEM((TILE, 2 * TILE), F32)] * U2,
+            pltpu.SMEM((2, FIRST + 384 + 128), jnp.int32),
             pltpu.SemaphoreType.DMA,
         ],
         compiler_params=pltpu.CompilerParams(vmem_limit_bytes=40 * 1024 * 1024),
@@ -252,10 +256,12 @@
 
 
 def greet(near):
-    barrier = pltpu.get_barrier_semaphore()
     for target in near.values():
-        pl.semaphore_signal(barrier, inc=1, device_id=target, device_id_type=MESH)
-    pl.semaphore_wait(barrier, len(near))
+        pl.semaphore_signal(pltpu.get_barrier_semaphore(), inc=1, device_id=target, device_id_type=MESH)
+
+
+def await_greetings(near):
+    pl.semaphore_wait(pltpu.get_barrier_semaphore(), len(near))
 
 
 class Copies:
@@ -286,7 +292,7 @@
 SCATTER_COPIES = 23
 
 
-def gather_kernel(pos_hbm, type_hbm, params_hbm, row_ref, col_ref, feat, mom, cen, vel, params_ref, pos_in, type_in, load_sem, send_sem, recv_sem):
+def gather_kernel(pos_hbm, type_hbm, params_hbm, row_ref, feat, mom, cen, vel, wid, table, col_ref, params_ref, pos_in, type_in, load_sem, send_sem, recv_sem):
     load_pos = pltpu.make_async_copy(pos_hbm, pos_in, load_sem.at[0])
     load_type = pltpu.make_async_copy(type_hbm, type_in, load_sem.at[1])
     load_params = pltpu.make_async_copy(params_hbm, params_ref, load_sem.at[2])
@@ -295,6 +301,7 @@
     load_params.start()
     y, zl, zh, x, core = place()
     near = neighbours(y, zl, zh, x, core)
+    greet(near)
     at = lambda xx, zz: core * 16 + zz * 4 + xx
     col_at = lambda yy, ll: yy * 2 + ll
     mine, col_mine, col_pal = at(x, zh), col_at(y, zl), col_at(y, 1 - zl)
@@ -304,7 +311,7 @@
         ref[slot, 0:3, :] = pos_in[...]
         for k in range(16):
             ref[slot, 3:4, k * TILE : (k + 1) * TILE] = type_in[k : k + 1, :].astype(F32)
-    greet(near)
+    await_greetings(near)
     net = Copies(near, send_sem, recv_sem)
 
     def send(ref, slot, to):
@@ -329,7 +336,11 @@
     pass_on(zh, "own")
     pass_col(col_mine, 0)
     load_params.wait()
-    prepare = column_preparer(params_ref, col_ref, feat, mom, cen, vel)
+    table[...] = jnp.zeros_like(table)
+    for k in range(4):
+        table[k : k + 1, 0:NTYPES] = jnp.sqrt(params_ref[0:1, :])
+        table[k + 4 : k + 5, 0:NTYPES] = params_ref[1:2, :] * WIDTH_SCALE
+    prepare = column_preparer(table, col_ref, feat, mom, cen, vel, wid)
     prepare(col_mine)
     pal.wait_recv()
     pass_col(col_pal, 1)
@@ -365,20 +376,22 @@
     hbm = pl.BlockSpec(memory_space=pltpu.HBM)
     vmem = pl.BlockSpec(memory_space=pltpu.VMEM)
     out = lambda *shape: jax.ShapeDtypeStruct(shape, F32)
-    row_data, _, *columns = pl.pallas_call(
+    row_data, *columns = pl.pallas_call(
         gather_kernel,
         out_shape=(
             out(32, 4, 2048),
-            out(8, 4, 2048),
             jax.ShapeDtypeStruct((COL_TILES, TILE, TILE), BF16),
-            jax.ShapeDtypeStruct((COL_TILES, 16, TILE), BF16),
             out(COL_TILES, 8, TILE),
             out(COL_TILES, 8, TILE),
-            out(2, NTYPES),
+            out(COL_TILES, 8, TILE),
+            out(COL_TILES, TILE, TILE),
+            out(8, TILE),
         ),
         in_specs=[hbm] * 3,
         out_specs=(vmem,) * 7,
         scratch_shapes=[
+            pltpu.VMEM((8, 4, 2048), F32),
+            pltpu.VMEM((2, NTYPES), F32),
             pltpu.VMEM((3, 2048), F32),
             pltpu.VMEM((16, TILE), jnp.int32),
             pltpu.SemaphoreType.DMA((3,)),
@@ -386,7 +399,7 @@
             pltpu.SemaphoreType.DMA((GATHER_COPIES,)),
         ],
         compiler_params=pltpu.CompilerParams(
-            collective_id=0, has_side_effects=True, vmem_limit_bytes=24 * 1024 * 1024
+            collective_id=0, has_side_effects=True, vmem_limit_bytes=32 * 1024 * 1024
         ),
         name="gather_atoms",
     )(*map(in_hbm, (positions, kinds, params)))
@@ -397,6 +410,7 @@
     y, zl, zh, x, core = place()
     near = neighbours(y, zl, zh, x, core)
     greet(near)
+    await_greetings(near)
     net = Copies(near, send_sem, recv_sem)
     offsets = (2, 1, -1, 0)
     order = ("far", "up", "down")

time: 63.9 us -> 68.5 us (1.072)
  local copies, waits for them, and re-layouts: 0.62 us -> 3.84 us
  Pallas kernels: 62.5 us -> 63.8 us
    unnamed x1 -> x3, local copies, waits for them, and re-layouts: 0.62 us -> 3.84 us
    pallas_call x1, Pallas kernels: 12.8 us -> 14.1 us  [scatter(): pl.pallas_call(scatter_kernel, out_shape=jax.ShapeDtypeStruct((3, 2048),...]
    pallas_call x1, Pallas kernels: 24.1 us -> 23.2 us  [gather(): pl.pallas_call(gather_kernel, out_shape=(out(32, 4, 2048), jax.ShapeDtype...]
    pallas_call x1, Pallas kernels: 25.7 us -> 26.5 us  [forces_of(): pl.pallas_call(force_kernel, out_shape=(jax.ShapeDtypeStruct((32, 48, TIL...]
where the time goes in v4:
time: 68.5 us; the launch traced here: 68.3 us
  Pallas kernels  63.8 us (93%)
  local copies, waits for them, and re-layouts  3.84 us (6%)
    pallas_call x1, Pallas kernels, forces_of(): pl.pallas_call(force_kernel, out_shape=(jax.ShapeDtypeStruct((32, 48, TIL...  26.5 us
    pallas_call x1, Pallas kernels, gather(): pl.pallas_call(gather_kernel, out_shape=(out(32, 4, 2048), jax.ShapeDtype...  23.2 us
    pallas_call x1, Pallas kernels, scatter(): pl.pallas_call(scatter_kernel, out_shape=jax.ShapeDtypeStruct((3, 2048),...  14.1 us
    unnamed x3, local copies, waits for them, and re-layouts  3.84 us

profile of v4, /device:TPU:1, one launch (start us, length us, event | category | flops | bytes accessed | tf_op | source)
XLA Modules:
  0.0 68.3 jit_solution(3842641526324878248)
XLA Ops:
  0.7 23.2 %gather_atoms.1 = (f32[32,4,2048]{2,1,0:T(4,128)S(1)}, bf16[128,128,128]{2,1,0:T(8,128)(2,1)S(1)}, f32[128,8,128]{2,1,0:T(8,128)S(1)}, f32[128,8,128]{2,1,0:T(8,...) custom-call(f32[3,2048]{1,0:T(4,128)} %pos_hbm.1, s32[16,128]{1,0:T(8,128)} %bitcast.4, ...), custom_call_target="tpu_custom_call" | custom-call | tf_op jit(solution)/shard_map/gather_atoms/pallas_call | solution.py:379
  23.9 0.0 copy-start
  23.9 3.2 %copy-done = f32[128,128,128]{2,1,0:T(8,128)} copy-done((f32[128,128,128]{2,1,0:T(8,128)}, f32[128,128,128]{2,1,0:T(8,128)S(1)}, u32[]{:S(2)}) %copy-start) | copy-done | bytes 8388632
  27.1 26.5 %pair_forces.1 = (f32[32,48,128]{2,1,0:T(8,128)S(1)}, f32[8,48,128]{2,1,0:T(8,128)S(1)}) custom-call(s32[1,1]{1,0:T(1,128)S(6)} %copy.7.count_ref, s32[2,384]{1,0:T(2,128)} %bitcast.5, f32[32,4,2048]{2,1,0:T(4,128)S(1)} %get-tuple-element.14.row_ref, bf16[128,128,128]{2,1,0:T(8,128)(2,1)S(1)} %get-tuple-element.15.feat, ...), custom_call_target="tpu_custom_call" | custom-call | tf_op jit(solution)/shard_map/pair_forces/pallas_call | solution.py:211
  53.6 14.1 %scatter_forces.1 = f32[3,2048]{1,0:T(4,128)S(1)} custom-call(f32[32,48,128]{2,1,0:T(8,128)S(1)} %get-tuple-element.21.row_ref, f32[8,48,128]{2,1,0:T(8,128)S(1)} %get-tuple-element.22.col_ref), custom_call_target="tpu_custom_call" | custom-call | tf_op jit(solution)/shard_map/scatter_forces/pallas_call | solution.py:464
  67.7 0.6 copy.8
Async XLA Ops:
  23.9 3.2 %copy-start = (f32[128,128,128]{2,1,0:T(8,128)}, f32[128,128,128]{2,1,0:T(8,128)S(1)}, u32[]{:S(2)}) copy-start(f32[128,128,128]{2,1,0:T(8,128)S(1)} %get-tuple-element.19.wid) | copy-start | bytes 25165828

commit v5 on v4

--- a/solution.py
+++ b/solution.py
@@ -225,7 +225,7 @@
             pltpu.SMEM((2, FIRST + 384 + 128), jnp.int32),
             pltpu.SemaphoreType.DMA,
         ],
-        compiler_params=pltpu.CompilerParams(vmem_limit_bytes=40 * 1024 * 1024),
+        compiler_params=pltpu.CompilerParams(vmem_limit_bytes=26 * 1024 * 1024),
         name="pair_forces",
     )(count, tiles, row_data, *columns)
 
@@ -399,7 +399,7 @@
             pltpu.SemaphoreType.DMA((GATHER_COPIES,)),
         ],
         compiler_params=pltpu.CompilerParams(
-            collective_id=0, has_side_effects=True, vmem_limit_bytes=32 * 1024 * 1024
+            collective_id=0, has_side_effects=True, vmem_limit_bytes=22 * 1024 * 1024
         ),
         name="gather_atoms",
     )(*map(in_hbm, (positions, kinds, params)))
@@ -479,7 +479,7 @@
             pltpu.SemaphoreType.DMA((SCATTER_COPIES,)),
         ],
         compiler_params=pltpu.CompilerParams(
-            collective_id=1, has_side_effects=True, vmem_limit_bytes=16 * 1024 * 1024
+            collective_id=1, has_side_effects=True, vmem_limit_bytes=10 * 1024 * 1024
         ),
         name="scatter_forces",
     )(row_part, col_part)

time: 68.5 us -> 59.9 us (0.87)
  Pallas kernels: 63.8 us -> 58.1 us
  local copies, waits for them, and re-layouts: 3.84 us -> 0.62 us
    pallas_call x1, Pallas kernels: 26.5 us -> 12.8 us  [forces_of(): pl.pallas_call(force_kernel, out_shape=(jax.ShapeDtypeStruct((32, 48, TIL...]
    pallas_call x1, Pallas kernels: 14.1 us -> 22 us  [scatter(): pl.pallas_call(scatter_kernel, out_shape=jax.ShapeDtypeStruct((3, 2048),...]
    unnamed x3 -> x1, local copies, waits for them, and re-layouts: 3.84 us -> 0.62 us
where the time goes in v5:
time: 59.9 us; the launch traced here: 59.4 us
  Pallas kernels  58.1 us (97%)
  between operations  0.68 us (1%)
  local copies, waits for them, and re-layouts  0.62 us (1%)
    pallas_call x1, Pallas kernels, gather(): pl.pallas_call(gather_kernel, out_shape=(out(32, 4, 2048), jax.ShapeDtype...  23.2 us
    pallas_call x1, Pallas kernels, scatter(): pl.pallas_call(scatter_kernel, out_shape=jax.ShapeDtypeStruct((3, 2048),...  22 us
    pallas_call x1, Pallas kernels, forces_of(): pl.pallas_call(force_kernel, out_shape=(jax.ShapeDtypeStruct((32, 48, TIL...  12.8 us

profile of v5, /device:TPU:1, one launch (start us, length us, event | category | flops | bytes accessed | tf_op | source)
XLA Modules:
  0.0 59.4 jit_solution(12844997220348721831)
XLA Ops:
  0.7 23.2 %gather_atoms.1 = (f32[32,4,2048]{2,1,0:T(4,128)S(1)}, bf16[128,128,128]{2,1,0:T(8,128)(2,1)S(1)}, f32[128,8,128]{2,1,0:T(8,128)S(1)}, f32[128,8,128]{2,1,0:T(8,...) custom-call(f32[3,2048]{1,0:T(4,128)} %pos_hbm.1, s32[16,128]{1,0:T(8,128)} %bitcast.4, ...), custom_call_target="tpu_custom_call" | custom-call | tf_op jit(solution)/shard_map/gather_atoms/pallas_call | solution.py:379
  23.9 12.8 %pair_forces.1 = (f32[32,48,128]{2,1,0:T(8,128)S(1)}, f32[8,48,128]{2,1,0:T(8,128)S(1)}) custom-call(s32[1,1]{1,0:T(1,128)S(6)} %copy.7.count_ref, s32[2,384]{1,0:T(2,128)} %bitcast.5, f32[32,4,2048]{2,1,0:T(4,128)S(1)} %get-tuple-element.14.row_ref, bf16[128,128,128]{2,1,0:T(8,128)(2,1)S(1)} %get-tuple-element.15.feat, ...), custom_call_target="tpu_custom_call" | custom-call | tf_op jit(solution)/shard_map/pair_forces/pallas_call | solution.py:211
  36.7 22.0 %scatter_forces.1 = f32[3,2048]{1,0:T(4,128)S(1)} custom-call(f32[32,48,128]{2,1,0:T(8,128)S(1)} %get-tuple-element.21.row_ref, f32[8,48,128]{2,1,0:T(8,128)S(1)} %get-tuple-element.22.col_ref), custom_call_target="tpu_custom_call" | custom-call | tf_op jit(solution)/shard_map/scatter_forces/pallas_call | solution.py:464
  58.8 0.6 %copy.8 = f32[3,2048]{1,0:T(4,128)} copy(f32[3,2048]{1,0:T(4,128)S(1)} %scatter_forces.1) | data formatting | bytes 49152

commit v6 on v5

--- a/solution.py
+++ b/solution.py
@@ -14,7 +14,8 @@
 KAPPA = 2.0 / (CUTOFF_SQ * LOG2E)
 WIDTH_SCALE = 0.5 / math.sqrt(CUTOFF_SQ * LOG2E)
 GROUP = 8
-TURNS = 4
+TURNS = 5
+CHUNK = 32
 UNROLL = GROUP * TURNS
 G2 = 2 * GROUP
 U2 = GROUP
@@ -142,16 +143,16 @@
     def spread_out(slot, k):
         b = tiles_ref[1, slot] & (COL_TILES - 1)
         half = (k % 2) * TILE
-        c = jnp.maximum(reach[k // 2 % U2][:, half : half + TILE], 0.0)
-        spans = wid[b].reshape(16, 8, TILE) + span[k][...][None]
-        inverse = pl.reciprocal(spans.reshape(TILE, TILE), approx=True)
-        decay = inverse * inverse
-        u = c * decay
-        g = (c * (u + 2.0 * LOG2E)) * jnp.exp2(u - decay)
-        g_high = g.astype(BF16)
-        g_low = (g - g_high.astype(F32)).astype(BF16)
-        slope[k % G2][0:TILE, :] = g_high
-        slope[k % G2][TILE : 2 * TILE, :] = g_low
+        for low in range(0, TILE, CHUNK):
+            c = jnp.maximum(reach[k // 2 % U2][low : low + CHUNK, half : half + TILE], 0.0)
+            spans = wid[b, low : low + CHUNK, :].reshape(CHUNK // 8, 8, TILE) + span[k][...][None]
+            inverse = pl.reciprocal(spans.reshape(CHUNK, TILE), approx=True)
+            decay = inverse * inverse
+            u = c * decay
+            g = (c * (u + 2.0 * LOG2E)) * jnp.exp2(u - decay)
+            g_high = g.astype(BF16)
+            slope[k % G2][low : low + CHUNK, :] = g_high
+            slope[k % G2][TILE + low : TILE + low + CHUNK, :] = (g - g_high.astype(F32)).astype(BF16)
 
     def gather_in(slot, k):
         a, b = tiles_ref[0, slot], tiles_ref[1, slot]
@@ -322,14 +323,15 @@
     pal = send(col_ref, col_mine, "pal")
 
     def pass_on(zz, key):
-        along_x[key] = {name: send(row_ref, at(x, zz), "x_" + name) for name in STEPS}
+        names = ("up", "down") if key in ("up", "down") else STEPS
+        along_x[key] = {name: send(row_ref, at(x, zz), "x_" + name) for name in names}
         twins.append(send(row_ref, at(x, zz), "twin"))
 
     def pass_col(slot, key):
         along_y[key] = {name: send(col_ref, slot, "y_" + name) for name in STEPS}
 
-    def hand_over(zz, key):
-        for name in ("up", "down", "far"):
+    def hand_over(zz, key, names):
+        for name in names:
             along_x[key][name].wait_recv()
             twins.append(send(row_ref, at(ring(x, -STEPS[name]), zz), "twin"))
 
@@ -344,22 +346,28 @@
     prepare(col_mine)
     pal.wait_recv()
     pass_col(col_pal, 1)
+    along_x["own"]["far"].wait_recv()
+    across = {name: send(row_ref, at(ring(x, 2), zh), "z_" + name) for name in ("up", "down")}
+    twins.append(send(row_ref, at(ring(x, 2), zh), "twin"))
     for name in ("up", "down"):
         along_z[name].wait_recv()
         pass_on(ring(zh, -STEPS[name]), name)
-    prepare(col_pal)
-    hand_over(zh, "own")
+    hand_over(zh, "own", ("up", "down"))
     along_z["far"].wait_recv()
     pass_on(ring(zh, 2), "far")
+    prepare(col_pal)
     for name in ("up", "down"):
         along_y[0][name].wait_recv()
         prepare(col_at(ring(y, -STEPS[name]), zl))
-    hand_over(ring(zh, -1), "up")
-    hand_over(ring(zh, 1), "down")
+    for name in ("up", "down"):
+        zz = ring(zh, -STEPS[name])
+        hand_over(zz, name, ("up", "down"))
+        across[name].wait_recv()
+        twins.append(send(row_ref, at(ring(x, 2), zz), "twin"))
     for name in ("up", "down"):
         along_y[1][name].wait_recv()
         prepare(col_at(ring(y, -STEPS[name]), 1 - zl))
-    hand_over(ring(zh, 2), "far")
+    hand_over(ring(zh, 2), "far", ("up", "down", "far"))
     for key, ll in ((0, zl), (1, 1 - zl)):
         along_y[key]["far"].wait_recv()
         prepare(col_at(ring(y, 2), ll))

time: 59.9 us -> 59.4 us (level)
    pallas_call x1, Pallas kernels: 12.8 us -> 21.6 us  [forces_of(): pl.pallas_call(force_kernel, out_shape=(jax.ShapeDtypeStruct((32, 48, TIL...]
    pallas_call x1, Pallas kernels: 22 us -> 13.9 us  [scatter(): pl.pallas_call(scatter_kernel, out_shape=jax.ShapeDtypeStruct((3, 2048),...]
    pallas_call x1, Pallas kernels: 23.2 us -> 22.5 us  [gather(): pl.pallas_call(gather_kernel, out_shape=(out(32, 4, 2048), jax.ShapeDtype...]
where the time goes in v6:
time: 59.4 us; the launch traced here: 59.2 us
  Pallas kernels  58 us (98%)
  between operations  0.68 us (1%)
  local copies, waits for them, and re-layouts  0.62 us (1%)
    pallas_call x1, Pallas kernels, gather(): pl.pallas_call(gather_kernel, out_shape=(out(32, 4, 2048), jax.ShapeDtype...  22.5 us
    pallas_call x1, Pallas kernels, forces_of(): pl.pallas_call(force_kernel, out_shape=(jax.ShapeDtypeStruct((32, 48, TIL...  21.6 us
    pallas_call x1, Pallas kernels, scatter(): pl.pallas_call(scatter_kernel, out_shape=jax.ShapeDtypeStruct((3, 2048),...  13.9 us

profile of v6, /device:TPU:1, one launch (start us, length us, event | category | flops | bytes accessed | tf_op | source)
XLA Modules:
  0.0 59.2 jit_solution(9612490655198946831)
XLA Ops:
  0.7 22.5 %gather_atoms.1 = (f32[32,4,2048]{2,1,0:T(4,128)S(1)}, bf16[128,128,128]{2,1,0:T(8,128)(2,1)S(1)}, f32[128,8,128]{2,1,0:T(8,128)S(1)}, f32[128,8,128]{2,1,0:T(8,...) custom-call(f32[3,2048]{1,0:T(4,128)} %pos_hbm.1, s32[16,128]{1,0:T(8,128)} %bitcast.4, ...), custom_call_target="tpu_custom_call" | custom-call | tf_op jit(solution)/shard_map/gather_atoms/pallas_call | solution.py:387
  23.1 21.6 %pair_forces.1 = (f32[32,48,128]{2,1,0:T(8,128)S(1)}, f32[8,48,128]{2,1,0:T(8,128)S(1)}) custom-call(s32[1,1]{1,0:T(1,128)S(6)} %copy.7.count_ref, s32[2,384]{1,0:T(2,128)} %bitcast.5, f32[32,4,2048]{2,1,0:T(4,128)S(1)} %get-tuple-element.14.row_ref, bf16[128,128,128]{2,1,0:T(8,128)(2,1)S(1)} %get-tuple-element.15.feat, ...), custom_call_target="tpu_custom_call" | custom-call | tf_op jit(solution)/shard_map/pair_forces/pallas_call | solution.py:212
  44.7 13.9 %scatter_forces.1 = f32[3,2048]{1,0:T(4,128)S(1)} custom-call(f32[32,48,128]{2,1,0:T(8,128)S(1)} %get-tuple-element.21.row_ref, f32[8,48,128]{2,1,0:T(8,128)S(1)} %get-tuple-element.22.col_ref), custom_call_target="tpu_custom_call" | custom-call | tf_op jit(solution)/shard_map/scatter_forces/pallas_call | solution.py:472
  58.6 0.6 %copy.8 = f32[3,2048]{1,0:T(4,128)} copy(f32[3,2048]{1,0:T(4,128)S(1)} %scatter_forces.1) | data formatting | bytes 49152

commit v7 on v6

--- a/solution.py
+++ b/solution.py
@@ -93,8 +93,8 @@
     return shard
 
 
-def force_kernel(count_ref, tiles_hbm, row_ref, feat, mom, cen, vel, wid, table, row_out, col_out, acc_row, acc_col, slope, mine, offset, scale, span, reach, tiles_ref, load_sem):
-    load_tiles = pltpu.make_async_copy(tiles_hbm, tiles_ref.at[:, pl.ds(FIRST, 384)], load_sem)
+def force_kernel(count_ref, tiles_in, row_ref, feat, mom, cen, vel, wid, table, row_out, col_out, acc_row, acc_col, slope, mine, offset, scale, span, reach, tiles_ref, load_sem):
+    load_tiles = pltpu.make_async_copy(tiles_in, tiles_ref.at[:, pl.ds(FIRST, 384)], load_sem)
     load_tiles.start()
     sub = lax.broadcasted_iota(jnp.int32, (8, TILE), 0)
     quad = sub & 3
@@ -186,9 +186,9 @@
                 if n % 2:
                     measure(base + h * GROUP + n - 1, h * GROUP + n - 1)
 
-    @pl.loop(0, COL_TILES, step=4)
+    @pl.loop(0, COL_TILES, step=16)
     def _(b0):
-        for k in range(4):
+        for k in range(16):
             b = b0 + k
             at = pl.multiple_of(b * 8, 8)
             got = acc_col[pl.ds(at, 8), :]
@@ -207,12 +207,11 @@
 
 
 def forces_of(count, tiles, row_data, *columns):
-    hbm = pl.BlockSpec(memory_space=pltpu.HBM)
     vmem = pl.BlockSpec(memory_space=pltpu.VMEM)
     return pl.pallas_call(
         force_kernel,
         out_shape=(jax.ShapeDtypeStruct((32, 48, TILE), F32), jax.ShapeDtypeStruct((8, 48, TILE), F32)),
-        in_specs=[pl.BlockSpec(memory_space=pltpu.SMEM), hbm] + [vmem] * 7,
+        in_specs=[pl.BlockSpec(memory_space=pltpu.SMEM)] + [vmem] * 8,
         out_specs=(vmem, vmem),
         scratch_shapes=[
             pltpu.VMEM(((ROW_TILES + 1) * 8, TILE), F32),
@@ -247,12 +246,14 @@
 STEPS = {"far": 2, "up": 1, "down": -1}
 
 
-def neighbours(y, zl, zh, x, core):
+def neighbours(y, zl, zh, x, core, cross=False):
     near = {"twin": device(y, zl, zh, x, 1 - core), "pal": device(y, 1 - zl, zh, x, core)}
     for name, d in STEPS.items():
         near["z_" + name] = device(y, zl, ring(zh, d), x, core)
         near["x_" + name] = device(y, zl, zh, ring(x, d), core)
         near["y_" + name] = device(ring(y, d), zl, zh, x, core)
+        if cross:
+            near["c_" + name] = device(y, zl, zh, ring(x, d), 1 - core)
     return near
 
 
@@ -290,16 +291,18 @@
 
 
 GATHER_COPIES = 38
-SCATTER_COPIES = 23
-
-
-def gather_kernel(pos_hbm, type_hbm, params_hbm, row_ref, feat, mom, cen, vel, wid, table, col_ref, params_ref, pos_in, type_in, load_sem, send_sem, recv_sem):
+SCATTER_COPIES = 26
+
+
+def gather_kernel(pos_hbm, type_hbm, params_hbm, tiles_hbm, tiles_ref, row_ref, feat, mom, cen, vel, wid, table, col_ref, params_ref, pos_in, type_in, load_sem, send_sem, recv_sem):
     load_pos = pltpu.make_async_copy(pos_hbm, pos_in, load_sem.at[0])
     load_type = pltpu.make_async_copy(type_hbm, type_in, load_sem.at[1])
     load_params = pltpu.make_async_copy(params_hbm, params_ref, load_sem.at[2])
     load_pos.start()
     load_type.start()
     load_params.start()
+    load_tiles = pltpu.make_async_copy(tiles_hbm, tiles_ref, load_sem.at[3])
+    load_tiles.start()
     y, zl, zh, x, core = place()
     near = neighbours(y, zl, zh, x, core)
     greet(near)
@@ -353,24 +356,27 @@
         along_z[name].wait_recv()
         pass_on(ring(zh, -STEPS[name]), name)
     hand_over(zh, "own", ("up", "down"))
+    prepare(col_pal)
+    along_y[0]["up"].wait_recv()
+    prepare(col_at(ring(y, -1), zl))
     along_z["far"].wait_recv()
     pass_on(ring(zh, 2), "far")
-    prepare(col_pal)
-    for name in ("up", "down"):
-        along_y[0][name].wait_recv()
-        prepare(col_at(ring(y, -STEPS[name]), zl))
+    along_y[0]["down"].wait_recv()
+    prepare(col_at(ring(y, 1), zl))
+    along_y[1]["up"].wait_recv()
+    prepare(col_at(ring(y, -1), 1 - zl))
     for name in ("up", "down"):
         zz = ring(zh, -STEPS[name])
         hand_over(zz, name, ("up", "down"))
         across[name].wait_recv()
         twins.append(send(row_ref, at(ring(x, 2), zz), "twin"))
-    for name in ("up", "down"):
-        along_y[1][name].wait_recv()
-        prepare(col_at(ring(y, -STEPS[name]), 1 - zl))
+    along_y[1]["down"].wait_recv()
+    prepare(col_at(ring(y, 1), 1 - zl))
     hand_over(ring(zh, 2), "far", ("up", "down", "far"))
     for key, ll in ((0, zl), (1, 1 - zl)):
         along_y[key]["far"].wait_recv()
         prepare(col_at(ring(y, 2), ll))
+    load_tiles.wait()
     for copy in twins:
         copy.wait_recv()
     net.finish()
@@ -380,13 +386,14 @@
     return pltpu.with_memory_space_constraint(array, pltpu.HBM)
 
 
-def gather(positions, kinds, params):
+def gather(positions, kinds, params, tiles):
     hbm = pl.BlockSpec(memory_space=pltpu.HBM)
     vmem = pl.BlockSpec(memory_space=pltpu.VMEM)
     out = lambda *shape: jax.ShapeDtypeStruct(shape, F32)
-    row_data, *columns = pl.pallas_call(
+    tiles, row_data, *columns = pl.pallas_call(
         gather_kernel,
         out_shape=(
+            jax.ShapeDtypeStruct((2, 384), jnp.int32),
             out(32, 4, 2048),
             jax.ShapeDtypeStruct((COL_TILES, TILE, TILE), BF16),
             out(COL_TILES, 8, TILE),
@@ -395,14 +402,14 @@
             out(COL_TILES, TILE, TILE),
             out(8, TILE),
         ),
-        in_specs=[hbm] * 3,
-        out_specs=(vmem,) * 7,
+        in_specs=[hbm] * 4,
+        out_specs=(vmem,) * 8,
         scratch_shapes=[
             pltpu.VMEM((8, 4, 2048), F32),
             pltpu.VMEM((2, NTYPES), F32),
             pltpu.VMEM((3, 2048), F32),
             pltpu.VMEM((16, TILE), jnp.int32),
-            pltpu.SemaphoreType.DMA((3,)),
+            pltpu.SemaphoreType.DMA((4,)),
             pltpu.SemaphoreType.DMA((GATHER_COPIES,)),
             pltpu.SemaphoreType.DMA((GATHER_COPIES,)),
         ],
@@ -410,32 +417,38 @@
             collective_id=0, has_side_effects=True, vmem_limit_bytes=22 * 1024 * 1024
         ),
         name="gather_atoms",
-    )(*map(in_hbm, (positions, kinds, params)))
-    return row_data, columns
-
-
-def scatter_kernel(row_ref, col_ref, out_ref, from_twin, row_sum, x_in, z_out, z_in, y_in, col_sum, pal_in, send_sem, recv_sem):
+    )(*map(in_hbm, (positions, kinds, params, tiles)))
+    return tiles, row_data, columns
+
+
+def scatter_kernel(row_ref, col_ref, out_ref, from_twin, row_sum, x_in, z_out, z_in, y_in, col_sum, pal_in, cross_in, send_sem, recv_sem):
     y, zl, zh, x, core = place()
-    near = neighbours(y, zl, zh, x, core)
+    near = neighbours(y, zl, zh, x, core, cross=True)
     greet(near)
     await_greetings(near)
     net = Copies(near, send_sem, recv_sem)
     offsets = (2, 1, -1, 0)
     order = ("far", "up", "down")
 
+    far = ring(zh, 2) * 4
+    along_x = [[]]
+    for k, n in enumerate(order):
+        there = far + ring(x, STEPS[n])
+        along_x[0].append(net.start(row_ref.at[core * 16 + there], x_in.at[0, k], "x_" + n))
+        along_x[0].append(net.start(row_ref.at[(1 - core) * 16 + there], cross_in.at[k], "c_" + n))
+    along_x[0].append(net.start(row_ref.at[(1 - core) * 16 + far + x], from_twin.at[far + x], "twin"))
     twins = []
-    for d in offsets:
+    for d in offsets[1:]:
         rows = ring(zh, d) * 4
         twins.append(net.start(row_ref.at[pl.ds((1 - core) * 16 + rows, 4)], from_twin.at[pl.ds(rows, 4)], "twin"))
     along_y = [net.start(col_ref.at[pl.ds(ring(y, STEPS[n]) * 2, 2)], y_in.at[k], "y_" + n) for k, n in enumerate(order)]
 
-    along_x = []
-    for i, d in enumerate(offsets):
+    for i, d in enumerate(offsets[1:]):
         rows = ring(zh, d) * 4
         twins[i].wait_recv()
         row_sum[pl.ds(rows, 4)] = row_ref[pl.ds(core * 16 + rows, 4)] + from_twin[pl.ds(rows, 4)]
         along_x.append(
-            [net.start(row_sum.at[rows + ring(x, STEPS[n])], x_in.at[i, k], "x_" + n) for k, n in enumerate(order)]
+            [net.start(row_sum.at[rows + ring(x, STEPS[n])], x_in.at[i + 1, k], "x_" + n) for k, n in enumerate(order)]
         )
 
     for copy in along_y:
@@ -449,7 +462,11 @@
     for i, d in enumerate(offsets):
         for copy in along_x[i]:
             copy.wait_recv()
-        total = row_sum[ring(zh, d) * 4 + x] + x_in[i, 0] + x_in[i, 1] + x_in[i, 2]
+        if d == 2:
+            total = row_ref[core * 16 + far + x] + from_twin[far + x] + cross_in[0] + cross_in[1] + cross_in[2]
+        else:
+            total = row_sum[ring(zh, d) * 4 + x]
+        total = total + x_in[i, 0] + x_in[i, 1] + x_in[i, 2]
         if d:
             z_out[i] = total
             along_z.append(net.start(z_out.at[i], z_in.at[i], "z_" + order[i]))
@@ -483,6 +500,7 @@
             block(3, 2),
             block(2),
             block(),
+            block(3),
             pltpu.SemaphoreType.DMA((SCATTER_COPIES,)),
             pltpu.SemaphoreType.DMA((SCATTER_COPIES,)),
         ],
@@ -494,9 +512,8 @@
 
 
 def shards(positions, type_ids, type_params, pair_tiles, pair_counts):
-    row_data, columns = gather(positions, type_ids.reshape(16, TILE), type_params)
-    tiles = pair_tiles[0, 0].T
-    row_part, col_part = forces_of(pair_counts, in_hbm(tiles), row_data, *columns)
+    tiles, row_data, columns = gather(positions, type_ids.reshape(16, TILE), type_params, pair_tiles[0, 0].T)
+    row_part, col_part = forces_of(pair_counts, tiles, row_data, *columns)
     return scatter(row_part, col_part)
 
 

time: 59.4 us -> 58.1 us (0.978)
  Pallas kernels: 58 us -> 57.2 us
    pallas_call x1, Pallas kernels: 21.6 us -> 5.21 us  [forces_of(): pl.pallas_call(force_kernel, out_shape=(jax.ShapeDtypeStruct((32, 48, TIL...]
    pallas_call x1, Pallas kernels: 13.9 us -> 29.5 us  [scatter(): pl.pallas_call(scatter_kernel, out_shape=jax.ShapeDtypeStruct((3, 2048),...]
where the time goes in v7:
time: 58.1 us; the launch traced here: 58.5 us
  Pallas kernels  57.2 us (98%)
  between operations  0.68 us (1%)
  local copies, waits for them, and re-layouts  0.62 us (1%)
    pallas_call x1, Pallas kernels, scatter(): pl.pallas_call(scatter_kernel, out_shape=jax.ShapeDtypeStruct((3, 2048),...  29.5 us
    pallas_call x1, Pallas kernels, gather(): pl.pallas_call(gather_kernel, out_shape=(jax.ShapeDtypeStruct((2, 384), j...  22.4 us
    pallas_call x1, Pallas kernels, forces_of(): pl.pallas_call(force_kernel, out_shape=(jax.ShapeDtypeStruct((32, 48, TIL...  5.21 us

profile of v7, /device:TPU:1, one launch (start us, length us, event | category | flops | bytes accessed | tf_op | source)
XLA Modules:
  0.0 58.5 jit_solution(679310190682164127)
XLA Ops:
  0.7 22.4 %gather_atoms.1 = (s32[2,384]{1,0:T(2,128)S(1)}, f32[32,4,2048]{2,1,0:T(4,128)S(1)}, bf16[128,128,128]{2,1,0:T(8,128)(2,1)S(1)}, f32[128,8,128]{2,1,0:T(8,128)S(...) custom-call(f32[3,2048]{1,0:T(4,128)} %pos_hbm.1, ...), custom_call_target="tpu_custom_call" | custom-call | tf_op jit(solution)/shard_map/gather_atoms/pallas_call | solution.py:393
  23.1 5.2 %pair_forces.1 = (f32[32,48,128]{2,1,0:T(8,128)S(1)}, f32[8,48,128]{2,1,0:T(8,128)S(1)}) custom-call(s32[1,1]{1,0:T(1,128)S(6)} %copy.7.count_ref, s32[2,384]{1,0:T(2,128)S(1)} %get-tuple-element.15.tiles_in, f32[32,4,2048]{2,1,0:T(4,128)S(1)} %get-tuple-element.16.row_ref, bf16[128,128,128]{2,1,0:T(8,128)(2,1)S(1)} %get-tuple-element.17.feat, ...), custom_call_target="tpu_custom_call" | custom-call | tf_op jit(solution)/shard_map/pair_forces/pallas_call | solution.py:211
  28.3 29.5 %scatter_forces.1 = f32[3,2048]{1,0:T(4,128)S(1)} custom-call(f32[32,48,128]{2,1,0:T(8,128)S(1)} %get-tuple-element.23.row_ref, f32[8,48,128]{2,1,0:T(8,128)S(1)} %get-tuple-element.24.col_ref), custom_call_target="tpu_custom_call" | custom-call | tf_op jit(solution)/shard_map/scatter_forces/pallas_call | solution.py:489
  57.8 0.6 %copy.8 = f32[3,2048]{1,0:T(4,128)} copy(f32[3,2048]{1,0:T(4,128)S(1)} %scatter_forces.1) | data formatting | bytes 49152

commit v8 on v7

--- a/solution.py
+++ b/solution.py
@@ -14,7 +14,7 @@
 KAPPA = 2.0 / (CUTOFF_SQ * LOG2E)
 WIDTH_SCALE = 0.5 / math.sqrt(CUTOFF_SQ * LOG2E)
 GROUP = 8
-TURNS = 5
+TURNS = 10
 CHUNK = 32
 UNROLL = GROUP * TURNS
 G2 = 2 * GROUP
@@ -107,7 +107,7 @@
     acc_col[...] = jnp.zeros_like(acc_col)
     load_tiles.wait()
     count = count_ref[0, 0]
-    for k in range(-2 * GROUP, 6 * GROUP):
+    for k in range(-2 * GROUP, (TURNS + 1) * GROUP):
         at = FIRST + k + (0 if k < 0 else count)
         tiles_ref[0, at] = ROW_TILES
         tiles_ref[1, at] = COL_TILES

time: 58.1 us -> 57.1 us (0.983); the launches traced: 58.5 us -> 56.7 us
  Pallas kernels: 57.2 us -> 55.4 us
    pallas_call x1, Pallas kernels: 29.5 us -> 24 us  [scatter(): pl.pallas_call(scatter_kernel, out_shape=jax.ShapeDtypeStruct((3, 2048),...]
    pallas_call x1, Pallas kernels: 5.21 us -> 9.03 us  [forces_of(): pl.pallas_call(force_kernel, out_shape=(jax.ShapeDtypeStruct((32, 48, TIL...]
where the time goes in v8:
time: 57.1 us; the launch traced here: 56.7 us
  Pallas kernels  55.4 us (97%)
  between operations  0.68 us (1%)
  local copies, waits for them, and re-layouts  0.62 us (1%)
    pallas_call x1, Pallas kernels, scatter(): pl.pallas_call(scatter_kernel, out_shape=jax.ShapeDtypeStruct((3, 2048),...  24 us
    pallas_call x1, Pallas kernels, gather(): pl.pallas_call(gather_kernel, out_shape=(jax.ShapeDtypeStruct((2, 384), j...  22.4 us
    pallas_call x1, Pallas kernels, forces_of(): pl.pallas_call(force_kernel, out_shape=(jax.ShapeDtypeStruct((32, 48, TIL...  9.03 us

profile of v8, /device:TPU:1, one launch (start us, length us, event | category | flops | bytes accessed | tf_op | source)
XLA Modules:
  0.0 56.7 jit_solution(3633027804366902919)
XLA Ops:
  0.7 22.4 %gather_atoms.1 = (s32[2,384]{1,0:T(2,128)S(1)}, f32[32,4,2048]{2,1,0:T(4,128)S(1)}, bf16[128,128,128]{2,1,0:T(8,128)(2,1)S(1)}, f32[128,8,128]{2,1,0:T(8,128)S(...) custom-call(f32[3,2048]{1,0:T(4,128)} %pos_hbm.1, ...), custom_call_target="tpu_custom_call" | custom-call | tf_op jit(solution)/shard_map/gather_atoms/pallas_call | solution.py:393
  23.1 9.0 %pair_forces.1 = (f32[32,48,128]{2,1,0:T(8,128)S(1)}, f32[8,48,128]{2,1,0:T(8,128)S(1)}) custom-call(s32[1,1]{1,0:T(1,128)S(6)} %copy.7.count_ref, s32[2,384]{1,0:T(2,128)S(1)} %get-tuple-element.15.tiles_in, f32[32,4,2048]{2,1,0:T(4,128)S(1)} %get-tuple-element.16.row_ref, bf16[128,128,128]{2,1,0:T(8,128)(2,1)S(1)} %get-tuple-element.17.feat, ...), custom_call_target="tpu_custom_call" | custom-call | tf_op jit(solution)/shard_map/pair_forces/pallas_call | solution.py:211
  32.1 24.0 %scatter_forces.1 = f32[3,2048]{1,0:T(4,128)S(1)} custom-call(f32[32,48,128]{2,1,0:T(8,128)S(1)} %get-tuple-element.23.row_ref, f32[8,48,128]{2,1,0:T(8,128)S(1)} %get-tuple-element.24.col_ref), custom_call_target="tpu_custom_call" | custom-call | tf_op jit(solution)/shard_map/scatter_forces/pallas_call | solution.py:489
  56.1 0.6 %copy.8 = f32[3,2048]{1,0:T(4,128)} copy(f32[3,2048]{1,0:T(4,128)S(1)} %scatter_forces.1) | data formatting | bytes 49152
